TPU v7x, 512 devices: a whole 4x4x16 slice. The times are simulated.
512 devices in a mesh: seq: 64 (over z, y_lo, core), head: 8 (over y_hi, x).
Axes of the slice: x: 4, y: 4 (y_hi: 2, y_lo: 2; y = y_hi * 2 + y_lo), z: 16, core: 2. Of those that a mesh axis runs over, the one named last changes fastest.
Arguments:
- query_rows: bfloat16 [16384, 4096], P('seq', 'head'), may hold values from -6 to 6
- key_rows: bfloat16 [16384, 1024], P('seq', 'head'), may hold values from -6 to 6
- value_rows: bfloat16 [16384, 1024], P('seq', 'head'), may hold values from -6 to 6
- out_weight: bfloat16 [4096, 4096], P('head'), may hold values from -0.125 to 0.125
- span_starts: int32 [64], replicated, may hold values from 0 to 16128, as said below
- round_masks: int32 [4], replicated, may hold values from 1 to 63, as said below
Outputs:
- projected: bfloat16 [16384, 4096], P('seq', 'head')
Inputs may be any that keep to these rules, and one draw needn't show every extreme that they name: `span_starts`: each multiple of 256 below 16384 stands exactly once. `round_masks`: distinct values; the first equals 63.
All inputs are finite; a program needn't handle non-finite values.
Results may differ from a plain program's by a relative error of at most 0.017.
Values may be sent and summed in bfloat16 or wider, within the bound.
No kernel may reach another device: no remote copies, remote signals or barrier semaphores. Data moves between devices by JAX's collectives and lax.ppermute only.
A program may use at most 64 MiB of HBM per device.

v0:
```python
import jax
import jax.numpy as jnp
from jax import lax
from jax.sharding import PartitionSpec as P

HD = 128
GROUP = 4


far_below = -1e30


def from_partner(x, axis, stride):
    return lax.ppermute(x, axis, [(i, i ^ 1 << stride) for i in range(lax.axis_size(axis))])


def attend_block(query_block, key_block, value_block, query_pos, key_pos):
    query_count = query_block.shape[0]
    key_count = key_block.shape[0]
    pair_heads = key_block.shape[1] // HD
    query_heads = query_block.reshape(query_count, pair_heads, GROUP, HD)
    key_heads = key_block.reshape(key_count, pair_heads, HD)
    value_heads = value_block.reshape(key_count, pair_heads, HD)
    scores = jnp.einsum(
        "tkgd,skd->kgts", query_heads, key_heads, preferred_element_type=jnp.float32
    ) * HD ** (-0.5)
    allowed = key_pos[None, :] <= query_pos[:, None]
    scores = jnp.where(allowed, scores, far_below)
    row_peak = jnp.max(scores, axis=-1)
    weights = jnp.where(allowed, jnp.exp(scores - row_peak[..., None]), 0.0)
    row_total = jnp.sum(weights, axis=-1)
    summed = jnp.einsum(
        "kgts,skd->tkgd",
        weights.astype(jnp.bfloat16),
        value_heads,
        preferred_element_type=jnp.float32,
    )
    return (row_peak, row_total, summed)


def empty_state(row_count, pair_heads):
    return (
        jnp.full((pair_heads, GROUP, row_count), far_below, jnp.float32),
        jnp.zeros((pair_heads, GROUP, row_count), jnp.float32),
        jnp.zeros((row_count, pair_heads, GROUP, HD), jnp.float32),
    )


def to_rows(stat):
    return jnp.transpose(stat, (2, 0, 1))[..., None]


def combine(earlier_state, later_state):
    row_peak = jnp.maximum(earlier_state[0], later_state[0])
    lift_a = jnp.exp(earlier_state[0] - row_peak)
    lift_b = jnp.exp(later_state[0] - row_peak)
    row_total = earlier_state[1] * lift_a + later_state[1] * lift_b
    summed = earlier_state[2] * to_rows(lift_a) + later_state[2] * to_rows(lift_b)
    return (row_peak, row_total, summed)


def bit_set(round_mask, bit_number):
    return jnp.bitwise_and(jnp.right_shift(round_mask, bit_number), 1) == 1


def fetch_pair(key_block, value_block, round_mask, bit_sequence):
    for bit_number in bit_sequence:
        moved_keys, moved_values = from_partner((key_block, value_block), "seq", bit_number)
        taking = bit_set(round_mask, bit_number)
        key_block = jnp.where(taking, moved_keys, key_block)
        value_block = jnp.where(taking, moved_values, value_block)
    return (key_block, value_block)


def per_device(query_rows, key_rows, value_rows, out_weight, span_starts, round_masks):
    rows_here = query_rows.shape[0]
    pair_heads = key_rows.shape[1] // HD
    own_index = lax.axis_index("seq")
    offsets = jnp.arange(rows_here, dtype=jnp.int32)
    own_start = span_starts[own_index]
    own_pos = own_start + offsets
    running_state = attend_block(query_rows, key_rows, value_rows, own_pos, own_pos)
    bit_count = lax.axis_size("seq").bit_length() - 1
    bit_sequence = list(range(bit_count))
    round_count = round_masks.shape[0]
    for round_index in range(round_count):
        round_mask = round_masks[round_index]
        partner_start = span_starts[jnp.bitwise_xor(own_index, round_mask)]
        far_keys, far_values = fetch_pair(key_rows, value_rows, round_mask, bit_sequence)

        def visiting():
            return attend_block(query_rows, far_keys, far_values, own_pos, partner_start + offsets)

        found = lax.cond(
            partner_start < own_start, visiting, lambda: empty_state(rows_here, pair_heads)
        )
        running_state = combine(running_state, found)
    attended = (
        (running_state[2] / to_rows(running_state[1])).reshape(rows_here, -1).astype(jnp.bfloat16)
    )
    placed = lax.psum_scatter(
        lax.dot_general(
            out_weight, attended, (((0,), (1,)), ((), ())), preferred_element_type=jnp.float32
        ).astype(jnp.bfloat16),
        "head",
        scatter_dimension=0,
        tiled=True,
    ).astype(jnp.float32)
    return placed.T.astype(jnp.bfloat16)


def solution(mesh):
    in_specs = (P("seq", "head"), P("seq", "head"), P("seq", "head"), P("head", None), P(), P())
    out_specs = P("seq", "head")
    return jax.shard_map(
        per_device, mesh=mesh, in_specs=in_specs, out_specs=out_specs, check_vma=False
    )
```

profile of v0, /device:TPU:1, one launch (start us, length us, event | category | flops | bytes accessed | tf_op | source)
XLA Modules:
  0.0 352.0 jit_solution(2108502660681847045)
XLA Ops:
  7.5 8.8 %collective-permute-start.6 = (bf16[256,128]{0,1:T(8,128)(2,1)S(1)}, bf16[256,128]{0,1:T(8,128)(2,1)S(1)}, u32[]{:S(2)}, u32[]{:S(2)}) collective-permute-start(bf16[256,128]{0,1:T(8,128)(2,1)S(1)} %copy.24), channel_id=1, source_target_pairs={{0,8},{8,0},{16,24},{24,16},{32,40},{40,32},{48,56},{56,48},{64,72... | collective-permute-start | bytes 196616 | tf_op jit(solution)/shard_map/ppermute | solution.py:14
  17.2 1.9 collective-permute-start
  23.1 1.5 fusion.113
  43.8 1.9 collective-permute-start.1
  45.7 3.4 collective-permute-start.32
  49.0 1.9 collective-permute-start.22
  51.0 3.4 collective-permute-start.12
  54.4 1.9 collective-permute-start.7
  56.3 3.4 collective-permute-start.37
  59.7 2.2 collective-permute-start.27
  62.0 3.1 collective-permute-start.17
  65.1 1.9 collective-permute-start.2
  67.0 3.4 collective-permute-start.33
  70.4 1.9 collective-permute-start.23
  72.4 3.4 collective-permute-start.13
  75.8 1.9 collective-permute-start.8
  77.8 3.4 collective-permute-start.38
  81.2 1.9 collective-permute-start.28
  83.1 3.4 collective-permute-start.18
  86.5 1.9 collective-permute-start.3
  88.5 4.3 %collective-permute-start.34 = (bf16[256,128]{0,1:T(8,128)(2,1)S(1)}, bf16[256,128]{0,1:T(8,128)(2,1)S(1)}, u32[]{:S(2)}, u32[]{:S(2)}) collective-permute-start(bf16[256,128]{0,1:T(8,128)(2,1)S(1)} %broadcast_select_fusion.5), channel_id=1, source_target_pairs={{0,64},{8,72},{16,80},{24,88},{32,96},{40,104},{48,112},{56,120},{... | collective-permute-start | bytes 196616 | tf_op jit(solution)/shard_map/ppermute | solution.py:14
  92.8 1.9 collective-permute-start.24
  94.7 4.3 %collective-permute-start.14 = (bf16[256,128]{0,1:T(8,128)(2,1)S(1)}, bf16[256,128]{0,1:T(8,128)(2,1)S(1)}, u32[]{:S(2)}, u32[]{:S(2)}) collective-permute-start(bf16[256,128]{0,1:T(8,128)(2,1)S(1)} %broadcast_select_fusion.25), channel_id=1, source_target_pairs={{0,64},{8,72},{16,80},{24,88},{32,96},{40,104},{48,112},{56,120},{... | collective-permute-start | bytes 196616 | tf_op jit(solution)/shard_map/ppermute | solution.py:14
  99.0 1.9 collective-permute-start.9
  101.0 4.3 %collective-permute-start.39 = (bf16[256,128]{0,1:T(8,128)(2,1)S(1)}, bf16[256,128]{0,1:T(8,128)(2,1)S(1)}, u32[]{:S(2)}, u32[]{:S(2)}) collective-permute-start(bf16[256,128]{0,1:T(8,128)(2,1)S(1)} %broadcast_select_fusion.4), channel_id=1, source_target_pairs={{0,64},{8,72},{16,80},{24,88},{32,96},{40,104},{48,112},{56,120},{... | collective-permute-start | bytes 196616 | tf_op jit(solution)/shard_map/ppermute | solution.py:14
  105.3 2.9 collective-permute-done.9
  108.2 1.9 collective-permute-start.29
  110.1 4.3 %collective-permute-start.19 = (bf16[256,128]{0,1:T(8,128)(2,1)S(1)}, bf16[256,128]{0,1:T(8,128)(2,1)S(1)}, u32[]{:S(2)}, u32[]{:S(2)}) collective-permute-start(bf16[256,128]{0,1:T(8,128)(2,1)S(1)} %broadcast_select_fusion.24), channel_id=1, source_target_pairs={{0,64},{8,72},{16,80},{24,88},{32,96},{40,104},{48,112},{56,120},{... | collective-permute-start | bytes 196616 | tf_op jit(solution)/shard_map/ppermute | solution.py:14
  114.4 4.2 %collective-permute-start.4 = (bf16[256,128]{0,1:T(8,128)(2,1)S(1)}, bf16[256,128]{0,1:T(8,128)(2,1)S(1)}, u32[]{:S(2)}, u32[]{:S(2)}) collective-permute-start(bf16[256,128]{0,1:T(8,128)(2,1)S(1)} %broadcast_select_fusion.37), channel_id=1, source_target_pairs={{0,128},{8,136},{16,144},{24,152},{32,160},{40,168},{48,176},{56,1... | collective-permute-start | bytes 196616 | tf_op jit(solution)/shard_map/ppermute | solution.py:14
  118.7 5.0 %collective-permute-start.35 = (bf16[256,128]{0,1:T(8,128)(2,1)S(1)}, bf16[256,128]{0,1:T(8,128)(2,1)S(1)}, u32[]{:S(2)}, u32[]{:S(2)}) collective-permute-start(bf16[256,128]{0,1:T(8,128)(2,1)S(1)} %broadcast_select_fusion.7), channel_id=1, source_target_pairs={{0,128},{8,136},{16,144},{24,152},{32,160},{40,168},{48,176},{56,1... | collective-permute-start | bytes 196616 | tf_op jit(solution)/shard_map/ppermute | solution.py:14
  123.7 4.2 %collective-permute-start.25 = (bf16[256,128]{0,1:T(8,128)(2,1)S(1)}, bf16[256,128]{0,1:T(8,128)(2,1)S(1)}, u32[]{:S(2)}, u32[]{:S(2)}) collective-permute-start(bf16[256,128]{0,1:T(8,128)(2,1)S(1)} %broadcast_select_fusion.17), channel_id=1, source_target_pairs={{0,128},{8,136},{16,144},{24,152},{32,160},{40,168},{48,176},{56,1... | collective-permute-start | bytes 196616 | tf_op jit(solution)/shard_map/ppermute | solution.py:14
  128.0 5.0 %collective-permute-start.15 = (bf16[256,128]{0,1:T(8,128)(2,1)S(1)}, bf16[256,128]{0,1:T(8,128)(2,1)S(1)}, u32[]{:S(2)}, u32[]{:S(2)}) collective-permute-start(bf16[256,128]{0,1:T(8,128)(2,1)S(1)} %broadcast_select_fusion.27), channel_id=1, source_target_pairs={{0,128},{8,136},{16,144},{24,152},{32,160},{40,168},{48,176},{56,1... | collective-permute-start | bytes 196616 | tf_op jit(solution)/shard_map/ppermute | solution.py:14
  133.0 4.2 %collective-permute-start.10 = (bf16[256,128]{0,1:T(8,128)(2,1)S(1)}, bf16[256,128]{0,1:T(8,128)(2,1)S(1)}, u32[]{:S(2)}, u32[]{:S(2)}) collective-permute-start(bf16[256,128]{0,1:T(8,128)(2,1)S(1)} %broadcast_select_fusion.36), channel_id=1, source_target_pairs={{0,128},{8,136},{16,144},{24,152},{32,160},{40,168},{48,176},{56,1... | collective-permute-start | bytes 196616 | tf_op jit(solution)/shard_map/ppermute | solution.py:14
  137.2 5.0 %collective-permute-start.40 = (bf16[256,128]{0,1:T(8,128)(2,1)S(1)}, bf16[256,128]{0,1:T(8,128)(2,1)S(1)}, u32[]{:S(2)}, u32[]{:S(2)}) collective-permute-start(bf16[256,128]{0,1:T(8,128)(2,1)S(1)} %broadcast_select_fusion.6), channel_id=1, source_target_pairs={{0,128},{8,136},{16,144},{24,152},{32,160},{40,168},{48,176},{56,1... | collective-permute-start | bytes 196616 | tf_op jit(solution)/shard_map/ppermute | solution.py:14
  142.2 15.9 %collective-permute-done.10 = bf16[256,128]{0,1:T(8,128)(2,1)S(1)} collective-permute-done((bf16[256,128]{0,1:T(8,128)(2,1)S(1)}, bf16[256,128]{0,1:T(8,128)(2,1)S(1)}, u32[]{:S(2)}, u32[]{:S(2)}) %collective-permute-start.10) | collective-permute-done | bytes 65568 | tf_op jit(solution)/shard_map/ppermute | solution.py:14
  158.2 1.9 collective-permute-start.30
  160.1 7.3 %collective-permute-start.20 = (bf16[256,128]{0,1:T(8,128)(2,1)S(1)}, bf16[256,128]{0,1:T(8,128)(2,1)S(1)}, u32[]{:S(2)}, u32[]{:S(2)}) collective-permute-start(bf16[256,128]{0,1:T(8,128)(2,1)S(1)} %broadcast_select_fusion.26), channel_id=1, source_target_pairs={{0,128},{8,136},{16,144},{24,152},{32,160},{40,168},{48,176},{56,1... | collective-permute-start | bytes 196616 | tf_op jit(solution)/shard_map/ppermute | solution.py:14
  167.4 9.6 %collective-permute-start.5 = (bf16[256,128]{0,1:T(8,128)(2,1)S(1)}, bf16[256,128]{0,1:T(8,128)(2,1)S(1)}, u32[]{:S(2)}, u32[]{:S(2)}) collective-permute-start(bf16[256,128]{0,1:T(8,128)(2,1)S(1)} %broadcast_select_fusion.39), channel_id=1, source_target_pairs={{0,256},{8,264},{16,272},{24,280},{32,288},{40,296},{48,304},{56,3... | collective-permute-start | bytes 196616 | tf_op jit(solution)/shard_map/ppermute | solution.py:14
  177.0 4.4 %collective-permute-start.36 = (bf16[256,128]{0,1:T(8,128)(2,1)S(1)}, bf16[256,128]{0,1:T(8,128)(2,1)S(1)}, u32[]{:S(2)}, u32[]{:S(2)}) collective-permute-start(bf16[256,128]{0,1:T(8,128)(2,1)S(1)} %broadcast_select_fusion.9), channel_id=1, source_target_pairs={{0,256},{8,264},{16,272},{24,280},{32,288},{40,296},{48,304},{56,3... | collective-permute-start | bytes 196616 | tf_op jit(solution)/shard_map/ppermute | solution.py:14
  181.5 9.6 %collective-permute-start.16 = (bf16[256,128]{0,1:T(8,128)(2,1)S(1)}, bf16[256,128]{0,1:T(8,128)(2,1)S(1)}, u32[]{:S(2)}, u32[]{:S(2)}) collective-permute-start(bf16[256,128]{0,1:T(8,128)(2,1)S(1)} %broadcast_select_fusion.29), channel_id=1, source_target_pairs={{0,256},{8,264},{16,272},{24,280},{32,288},{40,296},{48,304},{56,3... | collective-permute-start | bytes 196616 | tf_op jit(solution)/shard_map/ppermute | solution.py:14
  191.1 4.4 %collective-permute-start.11 = (bf16[256,128]{0,1:T(8,128)(2,1)S(1)}, bf16[256,128]{0,1:T(8,128)(2,1)S(1)}, u32[]{:S(2)}, u32[]{:S(2)}) collective-permute-start(bf16[256,128]{0,1:T(8,128)(2,1)S(1)} %broadcast_select_fusion.38), channel_id=1, source_target_pairs={{0,256},{8,264},{16,272},{24,280},{32,288},{40,296},{48,304},{56,3... | collective-permute-start | bytes 196616 | tf_op jit(solution)/shard_map/ppermute | solution.py:14
  195.6 9.6 %collective-permute-start.21 = (bf16[256,128]{0,1:T(8,128)(2,1)S(1)}, bf16[256,128]{0,1:T(8,128)(2,1)S(1)}, u32[]{:S(2)}, u32[]{:S(2)}) collective-permute-start(bf16[256,128]{0,1:T(8,128)(2,1)S(1)} %broadcast_select_fusion.28), channel_id=1, source_target_pairs={{0,256},{8,264},{16,272},{24,280},{32,288},{40,296},{48,304},{56,3... | collective-permute-start | bytes 196616 | tf_op jit(solution)/shard_map/ppermute | solution.py:14
  205.2 4.4 %collective-permute-start.26 = (bf16[256,128]{0,1:T(8,128)(2,1)S(1)}, bf16[256,128]{0,1:T(8,128)(2,1)S(1)}, u32[]{:S(2)}, u32[]{:S(2)}) collective-permute-start(bf16[256,128]{0,1:T(8,128)(2,1)S(1)} %broadcast_select_fusion.19), channel_id=1, source_target_pairs={{0,256},{8,264},{16,272},{24,280},{32,288},{40,296},{48,304},{56,3... | collective-permute-start | bytes 196616 | tf_op jit(solution)/shard_map/ppermute | solution.py:14
  210.6 9.8 %collective-permute-start.41 = (bf16[256,128]{0,1:T(8,128)(2,1)S(1)}, bf16[256,128]{0,1:T(8,128)(2,1)S(1)}, u32[]{:S(2)}, u32[]{:S(2)}) collective-permute-start(bf16[256,128]{0,1:T(8,128)(2,1)S(1)} %broadcast_select_fusion.8), channel_id=1, source_target_pairs={{0,256},{8,264},{16,272},{24,280},{32,288},{40,296},{48,304},{56,3... | collective-permute-start | bytes 196616 | tf_op jit(solution)/shard_map/ppermute | solution.py:14
  221.1 4.1 %collective-permute-start.31 = (bf16[256,128]{0,1:T(8,128)(2,1)S(1)}, bf16[256,128]{0,1:T(8,128)(2,1)S(1)}, u32[]{:S(2)}, u32[]{:S(2)}) collective-permute-start(bf16[256,128]{0,1:T(8,128)(2,1)S(1)} %broadcast_select_fusion.18), channel_id=1, source_target_pairs={{0,256},{8,264},{16,272},{24,280},{32,288},{40,296},{48,304},{56,3... | collective-permute-start | bytes 196616 | tf_op jit(solution)/shard_map/ppermute | solution.py:14
  227.3 8.1 %collective-permute-done.31 = bf16[256,128]{0,1:T(8,128)(2,1)S(1)} collective-permute-done((bf16[256,128]{0,1:T(8,128)(2,1)S(1)}, bf16[256,128]{0,1:T(8,128)(2,1)S(1)}, u32[]{:S(2)}, u32[]{:S(2)}) %collective-permute-start.31) | collective-permute-done | bytes 65568 | tf_op jit(solution)/shard_map/ppermute | solution.py:14
  240.3 2.7 fusion.72
  243.0 102.1 %reduce-scatter.2.cloned.1.call-done = bf16[512,256]{0,1:T(8,128)(2,1)} async-done(((bf16[4096,256]{0,1:T(8,128)(2,1)}), bf16[512,256]{0,1:T(8,128)(2,1)}) %reduce-scatter.2.cloned.1.call-update) | async-done | bytes 262160 | tf_op jit(solution)/shard_map/reduce_scatter | solution.py:101
  (118 shorter events, 17.0 us)
Async XLA Ops:
  6.5 338.6 %reduce-scatter.2.cloned.1.call-start = ((), (), s32[]{:S(2)}) async-start(), calls=%async_computation.1 | async-start | bytes 2359296 | tf_op jit(solution)/shard_map/reduce_scatter | solution.py:101
  7.5 46.9 %collective-permute-start.6 = (bf16[256,128]{0,1:T(8,128)(2,1)S(1)}, bf16[256,128]{0,1:T(8,128)(2,1)S(1)}, u32[]{:S(2)}, u32[]{:S(2)}) collective-permute-start(bf16[256,128]{0,1:T(8,128)(2,1)S(1)} %copy.24), channel_id=1, source_target_pairs={{0,8},{8,0},{16,24},{24,16},{32,40},{40,32},{48,56},{56,48},{64,72... | collective-permute-start | bytes 196616 | tf_op jit(solution)/shard_map/ppermute | solution.py:14
  17.2 26.5 %collective-permute-start = (bf16[256,128]{0,1:T(8,128)(2,1)S(1)}, bf16[256,128]{0,1:T(8,128)(2,1)S(1)}, u32[]{:S(2)}, u32[]{:S(2)}) collective-permute-start(bf16[256,128]{0,1:T(8,128)(2,1)S(1)} %copy.22), channel_id=1, source_target_pairs={{0,8},{8,0},{16,24},{24,16},{32,40},{40,32},{48,56},{56,48},{64,72... | collective-permute-start | bytes 196616 | tf_op jit(solution)/shard_map/ppermute | solution.py:14
  26.6 193.9 %copy-start = (bf16[256,512]{1,0:T(8,128)(2,1)S(1)}, bf16[256,512]{1,0:T(8,128)(2,1)}, u32[]{:S(2)}) copy-start(bf16[256,512]{1,0:T(8,128)(2,1)} %param.14) | copy-start | bytes 786436
  43.8 12.6 %collective-permute-start.1 = (bf16[256,128]{0,1:T(8,128)(2,1)S(1)}, bf16[256,128]{0,1:T(8,128)(2,1)S(1)}, u32[]{:S(2)}, u32[]{:S(2)}) collective-permute-start(bf16[256,128]{0,1:T(8,128)(2,1)S(1)} %get-tuple-element.355), channel_id=1, source_target_pairs={{0,16},{8,24},{16,0},{24,8},{32,48},{40,56},{48,32},{56,40},{64,80... | collective-permute-start | bytes 196616 | tf_op jit(solution)/shard_map/ppermute | solution.py:14
  45.7 16.3 %collective-permute-start.32 = (bf16[256,128]{0,1:T(8,128)(2,1)S(1)}, bf16[256,128]{0,1:T(8,128)(2,1)S(1)}, u32[]{:S(2)}, u32[]{:S(2)}) collective-permute-start(bf16[256,128]{0,1:T(8,128)(2,1)S(1)} %get-tuple-element.356), channel_id=1, source_target_pairs={{0,16},{8,24},{16,0},{24,8},{32,48},{40,56},{48,32},{56,40},{64,80... | collective-permute-start | bytes 196616 | tf_op jit(solution)/shard_map/ppermute | solution.py:14
  49.0 18.0 %collective-permute-start.22 = (bf16[256,128]{0,1:T(8,128)(2,1)S(1)}, bf16[256,128]{0,1:T(8,128)(2,1)S(1)}, u32[]{:S(2)}, u32[]{:S(2)}) collective-permute-start(bf16[256,128]{0,1:T(8,128)(2,1)S(1)} %get-tuple-element.357), channel_id=1, source_target_pairs={{0,16},{8,24},{16,0},{24,8},{32,48},{40,56},{48,32},{56,40},{64,80... | collective-permute-start | bytes 196616 | tf_op jit(solution)/shard_map/ppermute | solution.py:14
  51.0 19.5 %collective-permute-start.12 = (bf16[256,128]{0,1:T(8,128)(2,1)S(1)}, bf16[256,128]{0,1:T(8,128)(2,1)S(1)}, u32[]{:S(2)}, u32[]{:S(2)}) collective-permute-start(bf16[256,128]{0,1:T(8,128)(2,1)S(1)} %get-tuple-element.358), channel_id=1, source_target_pairs={{0,16},{8,24},{16,0},{24,8},{32,48},{40,56},{48,32},{56,40},{64,80... | collective-permute-start | bytes 196616 | tf_op jit(solution)/shard_map/ppermute | solution.py:14
  54.4 5.3 %collective-permute-start.7 = (bf16[256,128]{0,1:T(8,128)(2,1)S(1)}, bf16[256,128]{0,1:T(8,128)(2,1)S(1)}, u32[]{:S(2)}, u32[]{:S(2)}) collective-permute-start(bf16[256,128]{0,1:T(8,128)(2,1)S(1)} %get-tuple-element.351), channel_id=1, source_target_pairs={{0,16},{8,24},{16,0},{24,8},{32,48},{40,56},{48,32},{56,40},{64,80... | collective-permute-start | bytes 196616 | tf_op jit(solution)/shard_map/ppermute | solution.py:14
  56.3 8.7 %collective-permute-start.37 = (bf16[256,128]{0,1:T(8,128)(2,1)S(1)}, bf16[256,128]{0,1:T(8,128)(2,1)S(1)}, u32[]{:S(2)}, u32[]{:S(2)}) collective-permute-start(bf16[256,128]{0,1:T(8,128)(2,1)S(1)} %get-tuple-element.352), channel_id=1, source_target_pairs={{0,16},{8,24},{16,0},{24,8},{32,48},{40,56},{48,32},{56,40},{64,80... | collective-permute-start | bytes 196616 | tf_op jit(solution)/shard_map/ppermute | solution.py:14
  59.7 12.7 %collective-permute-start.27 = (bf16[256,128]{0,1:T(8,128)(2,1)S(1)}, bf16[256,128]{0,1:T(8,128)(2,1)S(1)}, u32[]{:S(2)}, u32[]{:S(2)}) collective-permute-start(bf16[256,128]{0,1:T(8,128)(2,1)S(1)} %get-tuple-element.353), channel_id=1, source_target_pairs={{0,16},{8,24},{16,0},{24,8},{32,48},{40,56},{48,32},{56,40},{64,80... | collective-permute-start | bytes 196616 | tf_op jit(solution)/shard_map/ppermute | solution.py:14
  62.0 13.8 %collective-permute-start.17 = (bf16[256,128]{0,1:T(8,128)(2,1)S(1)}, bf16[256,128]{0,1:T(8,128)(2,1)S(1)}, u32[]{:S(2)}, u32[]{:S(2)}) collective-permute-start(bf16[256,128]{0,1:T(8,128)(2,1)S(1)} %get-tuple-element.354), channel_id=1, source_target_pairs={{0,16},{8,24},{16,0},{24,8},{32,48},{40,56},{48,32},{56,40},{64,80... | collective-permute-start | bytes 196616 | tf_op jit(solution)/shard_map/ppermute | solution.py:14
  65.1 12.7 %collective-permute-start.2 = (bf16[256,128]{0,1:T(8,128)(2,1)S(1)}, bf16[256,128]{0,1:T(8,128)(2,1)S(1)}, u32[]{:S(2)}, u32[]{:S(2)}) collective-permute-start(bf16[256,128]{0,1:T(8,128)(2,1)S(1)} %broadcast_select_fusion.33), channel_id=1, source_target_pairs={{0,32},{8,40},{16,48},{24,56},{32,0},{40,8},{48,16},{56,24},{64,96... | collective-permute-start | bytes 196616 | tf_op jit(solution)/shard_map/ppermute | solution.py:14
  67.0 16.1 %collective-permute-start.33 = (bf16[256,128]{0,1:T(8,128)(2,1)S(1)}, bf16[256,128]{0,1:T(8,128)(2,1)S(1)}, u32[]{:S(2)}, u32[]{:S(2)}) collective-permute-start(bf16[256,128]{0,1:T(8,128)(2,1)S(1)} %broadcast_select_fusion.3), channel_id=1, source_target_pairs={{0,32},{8,40},{16,48},{24,56},{32,0},{40,8},{48,16},{56,24},{64,96... | collective-permute-start | bytes 196616 | tf_op jit(solution)/shard_map/ppermute | solution.py:14
  70.4 18.0 %collective-permute-start.23 = (bf16[256,128]{0,1:T(8,128)(2,1)S(1)}, bf16[256,128]{0,1:T(8,128)(2,1)S(1)}, u32[]{:S(2)}, u32[]{:S(2)}) collective-permute-start(bf16[256,128]{0,1:T(8,128)(2,1)S(1)} %broadcast_select_fusion.13), channel_id=1, source_target_pairs={{0,32},{8,40},{16,48},{24,56},{32,0},{40,8},{48,16},{56,24},{64,96... | collective-permute-start | bytes 196616 | tf_op jit(solution)/shard_map/ppermute | solution.py:14
  72.4 20.4 %collective-permute-start.13 = (bf16[256,128]{0,1:T(8,128)(2,1)S(1)}, bf16[256,128]{0,1:T(8,128)(2,1)S(1)}, u32[]{:S(2)}, u32[]{:S(2)}) collective-permute-start(bf16[256,128]{0,1:T(8,128)(2,1)S(1)} %broadcast_select_fusion.23), channel_id=1, source_target_pairs={{0,32},{8,40},{16,48},{24,56},{32,0},{40,8},{48,16},{56,24},{64,96... | collective-permute-start | bytes 196616 | tf_op jit(solution)/shard_map/ppermute | solution.py:14
  75.8 5.3 %collective-permute-start.8 = (bf16[256,128]{0,1:T(8,128)(2,1)S(1)}, bf16[256,128]{0,1:T(8,128)(2,1)S(1)}, u32[]{:S(2)}, u32[]{:S(2)}) collective-permute-start(bf16[256,128]{0,1:T(8,128)(2,1)S(1)} %broadcast_select_fusion.32), channel_id=1, source_target_pairs={{0,32},{8,40},{16,48},{24,56},{32,0},{40,8},{48,16},{56,24},{64,96... | collective-permute-start | bytes 196616 | tf_op jit(solution)/shard_map/ppermute | solution.py:14
  77.8 8.7 %collective-permute-start.38 = (bf16[256,128]{0,1:T(8,128)(2,1)S(1)}, bf16[256,128]{0,1:T(8,128)(2,1)S(1)}, u32[]{:S(2)}, u32[]{:S(2)}) collective-permute-start(bf16[256,128]{0,1:T(8,128)(2,1)S(1)} %broadcast_select_fusion.2), channel_id=1, source_target_pairs={{0,32},{8,40},{16,48},{24,56},{32,0},{40,8},{48,16},{56,24},{64,96... | collective-permute-start | bytes 196616 | tf_op jit(solution)/shard_map/ppermute | solution.py:14
  81.2 13.6 %collective-permute-start.28 = (bf16[256,128]{0,1:T(8,128)(2,1)S(1)}, bf16[256,128]{0,1:T(8,128)(2,1)S(1)}, u32[]{:S(2)}, u32[]{:S(2)}) collective-permute-start(bf16[256,128]{0,1:T(8,128)(2,1)S(1)} %broadcast_select_fusion.12), channel_id=1, source_target_pairs={{0,32},{8,40},{16,48},{24,56},{32,0},{40,8},{48,16},{56,24},{64,96... | collective-permute-start | bytes 196616 | tf_op jit(solution)/shard_map/ppermute | solution.py:14
  83.1 15.9 %collective-permute-start.18 = (bf16[256,128]{0,1:T(8,128)(2,1)S(1)}, bf16[256,128]{0,1:T(8,128)(2,1)S(1)}, u32[]{:S(2)}, u32[]{:S(2)}) collective-permute-start(bf16[256,128]{0,1:T(8,128)(2,1)S(1)} %broadcast_select_fusion.22), channel_id=1, source_target_pairs={{0,32},{8,40},{16,48},{24,56},{32,0},{40,8},{48,16},{56,24},{64,96... | collective-permute-start | bytes 196616 | tf_op jit(solution)/shard_map/ppermute | solution.py:14
  86.5 14.5 %collective-permute-start.3 = (bf16[256,128]{0,1:T(8,128)(2,1)S(1)}, bf16[256,128]{0,1:T(8,128)(2,1)S(1)}, u32[]{:S(2)}, u32[]{:S(2)}) collective-permute-start(bf16[256,128]{0,1:T(8,128)(2,1)S(1)} %broadcast_select_fusion.35), channel_id=1, source_target_pairs={{0,64},{8,72},{16,80},{24,88},{32,96},{40,104},{48,112},{56,120},{... | collective-permute-start | bytes 196616 | tf_op jit(solution)/shard_map/ppermute | solution.py:14
  88.5 21.7 %collective-permute-start.34 = (bf16[256,128]{0,1:T(8,128)(2,1)S(1)}, bf16[256,128]{0,1:T(8,128)(2,1)S(1)}, u32[]{:S(2)}, u32[]{:S(2)}) collective-permute-start(bf16[256,128]{0,1:T(8,128)(2,1)S(1)} %broadcast_select_fusion.5), channel_id=1, source_target_pairs={{0,64},{8,72},{16,80},{24,88},{32,96},{40,104},{48,112},{56,120},{... | collective-permute-start | bytes 196616 | tf_op jit(solution)/shard_map/ppermute | solution.py:14
  92.8 25.9 %collective-permute-start.24 = (bf16[256,128]{0,1:T(8,128)(2,1)S(1)}, bf16[256,128]{0,1:T(8,128)(2,1)S(1)}, u32[]{:S(2)}, u32[]{:S(2)}) collective-permute-start(bf16[256,128]{0,1:T(8,128)(2,1)S(1)} %broadcast_select_fusion.15), channel_id=1, source_target_pairs={{0,64},{8,72},{16,80},{24,88},{32,96},{40,104},{48,112},{56,120},{... | collective-permute-start | bytes 196616 | tf_op jit(solution)/shard_map/ppermute | solution.py:14
  94.7 29.0 %collective-permute-start.14 = (bf16[256,128]{0,1:T(8,128)(2,1)S(1)}, bf16[256,128]{0,1:T(8,128)(2,1)S(1)}, u32[]{:S(2)}, u32[]{:S(2)}) collective-permute-start(bf16[256,128]{0,1:T(8,128)(2,1)S(1)} %broadcast_select_fusion.25), channel_id=1, source_target_pairs={{0,64},{8,72},{16,80},{24,88},{32,96},{40,104},{48,112},{56,120},{... | collective-permute-start | bytes 196616 | tf_op jit(solution)/shard_map/ppermute | solution.py:14
  99.0 9.2 %collective-permute-start.9 = (bf16[256,128]{0,1:T(8,128)(2,1)S(1)}, bf16[256,128]{0,1:T(8,128)(2,1)S(1)}, u32[]{:S(2)}, u32[]{:S(2)}) collective-permute-start(bf16[256,128]{0,1:T(8,128)(2,1)S(1)} %broadcast_select_fusion.34), channel_id=1, source_target_pairs={{0,64},{8,72},{16,80},{24,88},{32,96},{40,104},{48,112},{56,120},{... | collective-permute-start | bytes 196616 | tf_op jit(solution)/shard_map/ppermute | solution.py:14
  101.0 13.4 %collective-permute-start.39 = (bf16[256,128]{0,1:T(8,128)(2,1)S(1)}, bf16[256,128]{0,1:T(8,128)(2,1)S(1)}, u32[]{:S(2)}, u32[]{:S(2)}) collective-permute-start(bf16[256,128]{0,1:T(8,128)(2,1)S(1)} %broadcast_select_fusion.4), channel_id=1, source_target_pairs={{0,64},{8,72},{16,80},{24,88},{32,96},{40,104},{48,112},{56,120},{... | collective-permute-start | bytes 196616 | tf_op jit(solution)/shard_map/ppermute | solution.py:14
  108.2 19.8 %collective-permute-start.29 = (bf16[256,128]{0,1:T(8,128)(2,1)S(1)}, bf16[256,128]{0,1:T(8,128)(2,1)S(1)}, u32[]{:S(2)}, u32[]{:S(2)}) collective-permute-start(bf16[256,128]{0,1:T(8,128)(2,1)S(1)} %broadcast_select_fusion.14), channel_id=1, source_target_pairs={{0,64},{8,72},{16,80},{24,88},{32,96},{40,104},{48,112},{56,120},{... | collective-permute-start | bytes 196616 | tf_op jit(solution)/shard_map/ppermute | solution.py:14
  110.1 22.8 %collective-permute-start.19 = (bf16[256,128]{0,1:T(8,128)(2,1)S(1)}, bf16[256,128]{0,1:T(8,128)(2,1)S(1)}, u32[]{:S(2)}, u32[]{:S(2)}) collective-permute-start(bf16[256,128]{0,1:T(8,128)(2,1)S(1)} %broadcast_select_fusion.24), channel_id=1, source_target_pairs={{0,64},{8,72},{16,80},{24,88},{32,96},{40,104},{48,112},{56,120},{... | collective-permute-start | bytes 196616 | tf_op jit(solution)/shard_map/ppermute | solution.py:14
  114.4 22.8 %collective-permute-start.4 = (bf16[256,128]{0,1:T(8,128)(2,1)S(1)}, bf16[256,128]{0,1:T(8,128)(2,1)S(1)}, u32[]{:S(2)}, u32[]{:S(2)}) collective-permute-start(bf16[256,128]{0,1:T(8,128)(2,1)S(1)} %broadcast_select_fusion.37), channel_id=1, source_target_pairs={{0,128},{8,136},{16,144},{24,152},{32,160},{40,168},{48,176},{56,1... | collective-permute-start | bytes 196616 | tf_op jit(solution)/shard_map/ppermute | solution.py:14
  118.7 41.4 %collective-permute-start.35 = (bf16[256,128]{0,1:T(8,128)(2,1)S(1)}, bf16[256,128]{0,1:T(8,128)(2,1)S(1)}, u32[]{:S(2)}, u32[]{:S(2)}) collective-permute-start(bf16[256,128]{0,1:T(8,128)(2,1)S(1)} %broadcast_select_fusion.7), channel_id=1, source_target_pairs={{0,128},{8,136},{16,144},{24,152},{32,160},{40,168},{48,176},{56,1... | collective-permute-start | bytes 196616 | tf_op jit(solution)/shard_map/ppermute | solution.py:14
  123.7 67.4 %collective-permute-start.25 = (bf16[256,128]{0,1:T(8,128)(2,1)S(1)}, bf16[256,128]{0,1:T(8,128)(2,1)S(1)}, u32[]{:S(2)}, u32[]{:S(2)}) collective-permute-start(bf16[256,128]{0,1:T(8,128)(2,1)S(1)} %broadcast_select_fusion.17), channel_id=1, source_target_pairs={{0,128},{8,136},{16,144},{24,152},{32,160},{40,168},{48,176},{56,1... | collective-permute-start | bytes 196616 | tf_op jit(solution)/shard_map/ppermute | solution.py:14
  128.0 49.0 %collective-permute-start.15 = (bf16[256,128]{0,1:T(8,128)(2,1)S(1)}, bf16[256,128]{0,1:T(8,128)(2,1)S(1)}, u32[]{:S(2)}, u32[]{:S(2)}) collective-permute-start(bf16[256,128]{0,1:T(8,128)(2,1)S(1)} %broadcast_select_fusion.27), channel_id=1, source_target_pairs={{0,128},{8,136},{16,144},{24,152},{32,160},{40,168},{48,176},{56,1... | collective-permute-start | bytes 196616 | tf_op jit(solution)/shard_map/ppermute | solution.py:14
  133.0 25.2 %collective-permute-start.10 = (bf16[256,128]{0,1:T(8,128)(2,1)S(1)}, bf16[256,128]{0,1:T(8,128)(2,1)S(1)}, u32[]{:S(2)}, u32[]{:S(2)}) collective-permute-start(bf16[256,128]{0,1:T(8,128)(2,1)S(1)} %broadcast_select_fusion.36), channel_id=1, source_target_pairs={{0,128},{8,136},{16,144},{24,152},{32,160},{40,168},{48,176},{56,1... | collective-permute-start | bytes 196616 | tf_op jit(solution)/shard_map/ppermute | solution.py:14
  137.2 30.2 %collective-permute-start.40 = (bf16[256,128]{0,1:T(8,128)(2,1)S(1)}, bf16[256,128]{0,1:T(8,128)(2,1)S(1)}, u32[]{:S(2)}, u32[]{:S(2)}) collective-permute-start(bf16[256,128]{0,1:T(8,128)(2,1)S(1)} %broadcast_select_fusion.6), channel_id=1, source_target_pairs={{0,128},{8,136},{16,144},{24,152},{32,160},{40,168},{48,176},{56,1... | collective-permute-start | bytes 196616 | tf_op jit(solution)/shard_map/ppermute | solution.py:14
  158.2 37.4 %collective-permute-start.30 = (bf16[256,128]{0,1:T(8,128)(2,1)S(1)}, bf16[256,128]{0,1:T(8,128)(2,1)S(1)}, u32[]{:S(2)}, u32[]{:S(2)}) collective-permute-start(bf16[256,128]{0,1:T(8,128)(2,1)S(1)} %broadcast_select_fusion.16), channel_id=1, source_target_pairs={{0,128},{8,136},{16,144},{24,152},{32,160},{40,168},{48,176},{56,1... | collective-permute-start | bytes 196616 | tf_op jit(solution)/shard_map/ppermute | solution.py:14
  160.1 21.4 %collective-permute-start.20 = (bf16[256,128]{0,1:T(8,128)(2,1)S(1)}, bf16[256,128]{0,1:T(8,128)(2,1)S(1)}, u32[]{:S(2)}, u32[]{:S(2)}) collective-permute-start(bf16[256,128]{0,1:T(8,128)(2,1)S(1)} %broadcast_select_fusion.26), channel_id=1, source_target_pairs={{0,128},{8,136},{16,144},{24,152},{32,160},{40,168},{48,176},{56,1... | collective-permute-start | bytes 196616 | tf_op jit(solution)/shard_map/ppermute | solution.py:14
  167.4 53.7 %collective-permute-start.5 = (bf16[256,128]{0,1:T(8,128)(2,1)S(1)}, bf16[256,128]{0,1:T(8,128)(2,1)S(1)}, u32[]{:S(2)}, u32[]{:S(2)}) collective-permute-start(bf16[256,128]{0,1:T(8,128)(2,1)S(1)} %broadcast_select_fusion.39), channel_id=1, source_target_pairs={{0,256},{8,264},{16,272},{24,280},{32,288},{40,296},{48,304},{56,3... | collective-permute-start | bytes 196616 | tf_op jit(solution)/shard_map/ppermute | solution.py:14
  177.0 59.0 %collective-permute-start.36 = (bf16[256,128]{0,1:T(8,128)(2,1)S(1)}, bf16[256,128]{0,1:T(8,128)(2,1)S(1)}, u32[]{:S(2)}, u32[]{:S(2)}) collective-permute-start(bf16[256,128]{0,1:T(8,128)(2,1)S(1)} %broadcast_select_fusion.9), channel_id=1, source_target_pairs={{0,256},{8,264},{16,272},{24,280},{32,288},{40,296},{48,304},{56,3... | collective-permute-start | bytes 196616 | tf_op jit(solution)/shard_map/ppermute | solution.py:14
  181.5 23.7 %collective-permute-start.16 = (bf16[256,128]{0,1:T(8,128)(2,1)S(1)}, bf16[256,128]{0,1:T(8,128)(2,1)S(1)}, u32[]{:S(2)}, u32[]{:S(2)}) collective-permute-start(bf16[256,128]{0,1:T(8,128)(2,1)S(1)} %broadcast_select_fusion.29), channel_id=1, source_target_pairs={{0,256},{8,264},{16,272},{24,280},{32,288},{40,296},{48,304},{56,3... | collective-permute-start | bytes 196616 | tf_op jit(solution)/shard_map/ppermute | solution.py:14
  191.1 34.2 %collective-permute-start.11 = (bf16[256,128]{0,1:T(8,128)(2,1)S(1)}, bf16[256,128]{0,1:T(8,128)(2,1)S(1)}, u32[]{:S(2)}, u32[]{:S(2)}) collective-permute-start(bf16[256,128]{0,1:T(8,128)(2,1)S(1)} %broadcast_select_fusion.38), channel_id=1, source_target_pairs={{0,256},{8,264},{16,272},{24,280},{32,288},{40,296},{48,304},{56,3... | collective-permute-start | bytes 196616 | tf_op jit(solution)/shard_map/ppermute | solution.py:14
  195.6 15.0 %collective-permute-start.21 = (bf16[256,128]{0,1:T(8,128)(2,1)S(1)}, bf16[256,128]{0,1:T(8,128)(2,1)S(1)}, u32[]{:S(2)}, u32[]{:S(2)}) collective-permute-start(bf16[256,128]{0,1:T(8,128)(2,1)S(1)} %broadcast_select_fusion.28), channel_id=1, source_target_pairs={{0,256},{8,264},{16,272},{24,280},{32,288},{40,296},{48,304},{56,3... | collective-permute-start | bytes 196616 | tf_op jit(solution)/shard_map/ppermute | solution.py:14
  205.2 22.1 %collective-permute-start.26 = (bf16[256,128]{0,1:T(8,128)(2,1)S(1)}, bf16[256,128]{0,1:T(8,128)(2,1)S(1)}, u32[]{:S(2)}, u32[]{:S(2)}) collective-permute-start(bf16[256,128]{0,1:T(8,128)(2,1)S(1)} %broadcast_select_fusion.19), channel_id=1, source_target_pairs={{0,256},{8,264},{16,272},{24,280},{32,288},{40,296},{48,304},{56,3... | collective-permute-start | bytes 196616 | tf_op jit(solution)/shard_map/ppermute | solution.py:14
  210.6 25.4 %collective-permute-start.41 = (bf16[256,128]{0,1:T(8,128)(2,1)S(1)}, bf16[256,128]{0,1:T(8,128)(2,1)S(1)}, u32[]{:S(2)}, u32[]{:S(2)}) collective-permute-start(bf16[256,128]{0,1:T(8,128)(2,1)S(1)} %broadcast_select_fusion.8), channel_id=1, source_target_pairs={{0,256},{8,264},{16,272},{24,280},{32,288},{40,296},{48,304},{56,3... | collective-permute-start | bytes 196616 | tf_op jit(solution)/shard_map/ppermute | solution.py:14
  221.1 4.2 %copy-start.4 = (f32[1,4,256]{2,1,0:T(4,128)}, f32[1,4,256]{2,1,0:T(4,128)S(1)}, u32[]{:S(2)}) copy-start(f32[1,4,256]{2,1,0:T(4,128)S(1)} %get-tuple-element.338) | copy-start | bytes 12292
  221.1 14.2 %collective-permute-start.31 = (bf16[256,128]{0,1:T(8,128)(2,1)S(1)}, bf16[256,128]{0,1:T(8,128)(2,1)S(1)}, u32[]{:S(2)}, u32[]{:S(2)}) collective-permute-start(bf16[256,128]{0,1:T(8,128)(2,1)S(1)} %broadcast_select_fusion.18), channel_id=1, source_target_pairs={{0,256},{8,264},{16,272},{24,280},{32,288},{40,296},{48,304},{56,3... | collective-permute-start | bytes 196616 | tf_op jit(solution)/shard_map/ppermute | solution.py:14
  226.0 9.4 %copy-start.5 = (f32[1,4,256]{2,1,0:T(4,128)}, f32[1,4,256]{2,1,0:T(4,128)S(1)}, u32[]{:S(2)}) copy-start(f32[1,4,256]{2,1,0:T(4,128)S(1)} %get-tuple-element.337) | copy-start | bytes 12292
  237.2 0.6 copy-start.7
  237.2 3.1 copy-start.1
  (1 other events, 0.6 us)
Sparse Core Ops, SparseCore 0:
  243.1 101.9 reduce-scatter.1
where the time goes:
time: 353 us; the launch traced here: 352 us
  starting transfers between devices  170 us (48%)
  waiting for transfers between devices  130 us (37%)
  between operations  33.8 us (10%)
  local copies, waits for them, and re-layouts  8.51 us (2%)
  matrix products  5.15 us (1%)
  other arithmetic  3.87 us (1%)
    ppermute x42, starting transfers between devices, from_partner(): lax.ppermute(x, axis, [(i, i ^ 1 << stride) for i in range(lax.axis_size(...  170 us
    reduce_scatter x1, waiting for transfers between devices, per_device(): lax.psum_scatter(lax.dot_general(out_weight, attended, (((0,), (1,)), (()...  102 us
    ppermute x42, waiting for transfers between devices, from_partner(): lax.ppermute(x, axis, [(i, i ^ 1 << stride) for i in range(lax.axis_size(...  28 us
  transfers between devices with their start and end apart: 43, of which 5 were waited for; matrix products, arithmetic and copies ran while one was open for 3% of the time, Pallas kernels for 0%

commit v1 on v0

v1 whole, which is shorter than its diff:
```python
import jax
import jax.numpy as jnp
from jax import lax
from jax.experimental import pallas as pl
from jax.experimental.pallas import tpu as pltpu
from jax.sharding import PartitionSpec as P

HD = 128
GROUP = 4
FAR_BELOW = -1e30
LOG2E = 1.4426950408889634


def attend_project(starts_ref, masks_ref, q_ref, kv_ref, f0, f1, f2, f3, w_ref, out_ref, peak, total, summed, attended):
    span = q_ref.shape[0]
    me = lax.axis_index("seq")
    own_start = starts_ref[me]

    def update(block, first, causal):
        keys = block[0:span, :]
        values = block[span : 2 * span, :]
        for h in range(GROUP):
            cols = slice(h * HD, (h + 1) * HD)
            scores = lax.dot_general(
                q_ref[:, cols], keys, (((1,), (1,)), ((), ())), preferred_element_type=jnp.float32
            ) * (HD ** (-0.5) * LOG2E)
            if causal:
                row = lax.broadcasted_iota(jnp.int32, scores.shape, 0)
                col = lax.broadcasted_iota(jnp.int32, scores.shape, 1)
                scores = jnp.where(col <= row, scores, FAR_BELOW)
            block_peak = jnp.max(scores, axis=1, keepdims=True)
            if first:
                new_peak = block_peak
            else:
                old_peak = peak[h, :, 0:1]
                new_peak = jnp.maximum(old_peak, block_peak)
            weights = jnp.exp2(scores - new_peak)
            block_total = jnp.sum(weights, axis=1, keepdims=True)
            block_sum = jnp.dot(weights.astype(jnp.bfloat16), values, preferred_element_type=jnp.float32)
            if not first:
                lift = jnp.exp2(old_peak - new_peak)
                block_total = block_total + total[h, :, 0:1] * lift
                block_sum = block_sum + summed[:, cols] * lift
            peak[h] = jnp.broadcast_to(new_peak, (span, HD))
            total[h] = jnp.broadcast_to(block_total, (span, HD))
            summed[:, cols] = block_sum

    @pl.when(pl.program_id(0) == 0)
    def _():
        update(kv_ref, True, True)
        for r, far in enumerate((f0, f1, f2, f3)):
            partner = jnp.bitwise_xor(me, masks_ref[r])

            @pl.when(starts_ref[partner] < own_start)
            def _(far=far):
                update(far, False, False)

        for h in range(GROUP):
            cols = slice(h * HD, (h + 1) * HD)
            attended[:, cols] = (summed[:, cols] / total[h]).astype(jnp.bfloat16)

    out_ref[0] = jnp.dot(attended[...], w_ref[...], preferred_element_type=jnp.float32).astype(jnp.bfloat16)


def add_shares(got_ref, out_ref):
    acc = got_ref[0].astype(jnp.float32)
    for j in range(1, got_ref.shape[0]):
        acc = acc + got_ref[j].astype(jnp.float32)
    out_ref[...] = acc.astype(out_ref.dtype)


def permuted(mask):
    return lambda x: lax.ppermute(x, "seq", [(i, i ^ mask) for i in range(lax.axis_size("seq"))])


def per_device(query_rows, key_rows, value_rows, out_weight, span_starts, round_masks):
    span, width = query_rows.shape
    heads = lax.axis_size("head")
    spans = lax.axis_size("seq")
    dout = out_weight.shape[1]
    cut = dout // heads
    kv = jnp.concatenate([key_rows, value_rows], axis=0)
    fars = [permuted(spans - 1)(kv)]
    for r in range(1, round_masks.shape[0]):
        fars.append(lax.switch(round_masks[r] - 1, [permuted(k) for k in range(1, spans - 1)], kv))

    whole = lambda shape: pl.BlockSpec(shape, lambda j, *_: (0,) * len(shape))
    shares = pl.pallas_call(
        attend_project,
        grid_spec=pltpu.PrefetchScalarGridSpec(
            num_scalar_prefetch=2,
            grid=(heads,),
            in_specs=[whole((span, width))]
            + [whole((2 * span, HD))] * 5
            + [pl.BlockSpec((width, cut), lambda j, *_: (0, j))],
            out_specs=pl.BlockSpec((1, span, cut), lambda j, *_: (j, 0, 0)),
            scratch_shapes=[
                pltpu.VMEM((GROUP, span, HD), jnp.float32),
                pltpu.VMEM((GROUP, span, HD), jnp.float32),
                pltpu.VMEM((span, width), jnp.float32),
                pltpu.VMEM((span, width), jnp.bfloat16),
            ],
        ),
        out_shape=jax.ShapeDtypeStruct((heads, span, cut), jnp.bfloat16),
        compiler_params=pltpu.CompilerParams(vmem_limit_bytes=32 * 2**20),
        cost_estimate=pl.CostEstimate(flops=3 * 2**30, bytes_accessed=8 * 2**20, transcendentals=2**21),
        name="attend_project",
    )(span_starts, round_masks, query_rows, kv, *fars, out_weight)
    got = lax.all_to_all(shares, "head", 0, 0, tiled=True)
    return pl.pallas_call(
        add_shares,
        grid=(4,),
        in_specs=[pl.BlockSpec((heads, span // 4, cut), lambda j: (0, j, 0))],
        out_specs=pl.BlockSpec((span // 4, cut), lambda j: (j, 0)),
        out_shape=jax.ShapeDtypeStruct((span, cut), jnp.bfloat16),
        compiler_params=pltpu.CompilerParams(vmem_limit_bytes=32 * 2**20),
        name="add_shares",
    )(got)


def solution(mesh):
    in_specs = (P("seq", "head"), P("seq", "head"), P("seq", "head"), P("head", None), P(), P())
    out_specs = P("seq", "head")
    return jax.shard_map(
        per_device, mesh=mesh, in_specs=in_specs, out_specs=out_specs, check_vma=False
    )
```

time: 353 us -> 177 us (0.50)
  starting transfers between devices: 170 us -> 63.8 us
  waiting for transfers between devices: 130 us -> 50.1 us
  blocking collectives: 0 us -> 34.5 us
  between operations: 33.8 us -> 1.81 us
  Pallas kernels: 0 us -> 18.7 us
  matrix products: 5.15 us -> 0 us
  other arithmetic: 3.87 us -> 0 us
    ppermute x42 -> x4, starting transfers between devices: 170 us -> 63.8 us  [permuted(): lax.ppermute(x, 'seq', [(i, i ^ mask) for i in range(lax.axis_size('seq'))])]
    reduce_scatter x1 -> x0, waiting for transfers between devices: 102 us -> none  [per_device(): lax.psum_scatter(lax.dot_general(out_weight, attended, (((0,), (1,)), (()...]
    all_to_all x0 -> x1, blocking collectives: none -> 34.5 us  [per_device(): got = lax.all_to_all(shares, 'head', 0, 0, tiled=True)]
    ppermute x42 -> x4, waiting for transfers between devices: 28 us -> 50.1 us  [permuted(): lax.ppermute(x, 'seq', [(i, i ^ mask) for i in range(lax.axis_size('seq'))])]
    pallas_call x0 -> x2, Pallas kernels: none -> 18.7 us  [the longest x1 17.1 us: per_device(): pl.pallas_call(attend_project, grid_spec=pltpu.PrefetchScalarGridSpec(num...]
    dot_general x3 -> x0, matrix products: 5.15 us -> none  [the longest x1 2.68 us: per_device(): lax.dot_general(out_weight, attended, (((0,), (1,)), ((), ())), preferred...]
  transfers between devices with their start and end apart: 43 -> 4, of which waited for: 5 -> 3; matrix products, arithmetic and copies ran while one was open for 3% -> 1% of each run, Pallas kernels for 0% -> 0%
where the time goes in v1:
time: 177 us
  starting transfers between devices  63.8 us (36%)
  waiting for transfers between devices  50.1 us (28%)
  blocking collectives  34.5 us (19%)
  Pallas kernels  18.7 us (11%)
  local copies, waits for them, and re-layouts  7.5 us (4%)
  between operations  1.81 us (1%)
    ppermute x4, starting transfers between devices, permuted(): lax.ppermute(x, 'seq', [(i, i ^ mask) for i in range(lax.axis_size('seq'))])  63.8 us
    ppermute x4, waiting for transfers between devices, permuted(): lax.ppermute(x, 'seq', [(i, i ^ mask) for i in range(lax.axis_size('seq'))])  50.1 us
    all_to_all x1, blocking collectives, per_device(): got = lax.all_to_all(shares, 'head', 0, 0, tiled=True)  34.5 us
    pallas_call x1, Pallas kernels, per_device(): pl.pallas_call(attend_project, grid_spec=pltpu.PrefetchScalarGridSpec(num...  17.1 us
    unnamed x9, local copies, waits for them, and re-layouts  5.29 us
  transfers between devices with their start and end apart: 4, of which 3 were waited for; matrix products, arithmetic and copies ran while one was open for 1% of the time, Pallas kernels for 0%

profile of v1, /device:TPU:1, one launch (start us, length us, event | category | flops | bytes accessed | tf_op | source)
XLA Modules:
  0.0 176.5 jit_solution(4632290623265687158)
XLA Ops:
  0.0 0.8 constant_dynamic-update-slice_fusion.1
  0.8 0.9 constant_dynamic-update-slice_fusion.kv_ref
  1.7 21.7 %collective-permute-start.186 = (bf16[512,128]{1,0:T(8,128)(2,1)S(1)}, bf16[512,128]{1,0:T(8,128)(2,1)S(1)}, u32[]{:S(2)}, u32[]{:S(2)}) collective-permute-start(bf16[512,128]{1,0:T(8,128)(2,1)S(1)} %constant_dynamic-update-slice_fusion.kv_ref), channel_id=1, source_target_pairs={{0,504},{8,496},{16,488},{24,480},{32,472},{40,464},{48,456},{56,4... | collective-permute-start | bytes 393224 | tf_op jit(solution)/shard_map/ppermute | solution.py:73
  23.4 1.4 fusion
  26.5 22.8 %conditional.5 = (bf16[512,128]{1,0:T(8,128)(2,1)}) conditional(s32[]{:T(128)} %bitcast.2, bf16[512,128]{1,0:T(8,128)(2,1)S(1)} %constant_dynamic-update-slice_fusion.kv_ref, bf16[512,128]{1,0:T(8,128)(2,1)S(1)} %constant_dynamic-update-slice_fusion.kv_ref, ...), branch_computations={%region_124.0_spmd, %region_125.0_spmd, %region_126.0_spmd, %regio... | conditional | bytes 524336 | solution.py:85
  26.6 12.8 %collective-permute-start.154 = (bf16[512,128]{1,0:T(8,128)(2,1)S(1)}, bf16[512,128]{1,0:T(8,128)(2,1)}, u32[]{:S(2)}, u32[]{:S(2)}) collective-permute-start(bf16[512,128]{1,0:T(8,128)(2,1)S(1)} %param.154), channel_id=1, source_target_pairs={{0,248},{8,240},{16,232},{24,224},{32,216},{40,208},{48,200},{56,1... | collective-permute-start | bytes 393224 | tf_op jit(solution)/shard_map/cond/branch_30_fun/ppermute | solution.py:73
  39.4 9.9 %collective-permute-done.154 = bf16[512,128]{1,0:T(8,128)(2,1)} collective-permute-done((bf16[512,128]{1,0:T(8,128)(2,1)S(1)}, bf16[512,128]{1,0:T(8,128)(2,1)}, u32[]{:S(2)}, u32[]{:S(2)}) %collective-permute-start.154) | collective-permute-done | bytes 131104 | tf_op jit(solution)/shard_map/cond/branch_30_fun/ppermute | solution.py:73
  49.3 28.0 %conditional.4 = (bf16[512,128]{1,0:T(8,128)(2,1)}) conditional(s32[]{:T(128)} %bitcast.1, bf16[512,128]{1,0:T(8,128)(2,1)S(1)} %constant_dynamic-update-slice_fusion.kv_ref, bf16[512,128]{1,0:T(8,128)(2,1)S(1)} %constant_dynamic-update-slice_fusion.kv_ref, ...), branch_computations={%region_62.0_spmd, %region_63.0_spmd, %region_64.0_spmd, %region_6... | conditional | bytes 524336 | solution.py:85
  49.3 12.3 %collective-permute-start.103 = (bf16[512,128]{1,0:T(8,128)(2,1)S(1)}, bf16[512,128]{1,0:T(8,128)(2,1)}, u32[]{:S(2)}, u32[]{:S(2)}) collective-permute-start(bf16[512,128]{1,0:T(8,128)(2,1)S(1)} %param.103), channel_id=1, source_target_pairs={{0,336},{8,344},{16,320},{24,328},{32,368},{40,376},{48,352},{56,3... | collective-permute-start | bytes 393224 | tf_op jit(solution)/shard_map/cond/branch_41_fun/ppermute | solution.py:73
  61.7 15.7 %collective-permute-done.103 = bf16[512,128]{1,0:T(8,128)(2,1)} collective-permute-done((bf16[512,128]{1,0:T(8,128)(2,1)S(1)}, bf16[512,128]{1,0:T(8,128)(2,1)}, u32[]{:S(2)}, u32[]{:S(2)}) %collective-permute-start.103) | collective-permute-done | bytes 131104 | tf_op jit(solution)/shard_map/cond/branch_41_fun/ppermute | solution.py:73
  77.4 41.5 %conditional.3 = (bf16[512,128]{1,0:T(8,128)(2,1)}) conditional(s32[]{:T(128)} %bitcast, bf16[512,128]{1,0:T(8,128)(2,1)S(1)} %constant_dynamic-update-slice_fusion.kv_ref, bf16[512,128]{1,0:T(8,128)(2,1)S(1)} %constant_dynamic-update-slice_fusion.kv_ref, ...), branch_computations={%region_0.0_spmd, %region_1.0_spmd, %region_2.0_spmd, %region_3.0_... | conditional | bytes 524336 | solution.py:85
  77.4 16.9 %collective-permute-start.37 = (bf16[512,128]{1,0:T(8,128)(2,1)S(1)}, bf16[512,128]{1,0:T(8,128)(2,1)}, u32[]{:S(2)}, u32[]{:S(2)}) collective-permute-start(bf16[512,128]{1,0:T(8,128)(2,1)S(1)} %param.37), channel_id=1, source_target_pairs={{0,304},{8,312},{16,288},{24,296},{32,272},{40,280},{48,256},{56,2... | collective-permute-start | bytes 393224 | tf_op jit(solution)/shard_map/cond/branch_37_fun/ppermute | solution.py:73
  94.3 24.5 %collective-permute-done.37 = bf16[512,128]{1,0:T(8,128)(2,1)} collective-permute-done((bf16[512,128]{1,0:T(8,128)(2,1)S(1)}, bf16[512,128]{1,0:T(8,128)(2,1)}, u32[]{:S(2)}, u32[]{:S(2)}) %collective-permute-start.37) | collective-permute-done | bytes 131104 | tf_op jit(solution)/shard_map/cond/branch_37_fun/ppermute | solution.py:73
  118.9 0.0 collective-permute-done.186.f0
  118.9 0.0 copy-start
  118.9 0.7 copy-done
  119.5 0.0 copy-start.1
  119.5 2.2 %copy-done.1 = bf16[512,4096]{1,0:T(8,128)(2,1)S(1)} copy-done((bf16[512,4096]{1,0:T(8,128)(2,1)S(1)}, bf16[512,4096]{1,0:T(8,128)(2,1)}, u32[]{:S(2)}) %copy-start.1) | copy-done | bytes 4194328
  121.7 0.0 copy-start.2
  121.7 0.9 copy-done.2
  122.7 0.0 copy-start.3
  122.7 0.7 copy-done.3
  123.3 17.1 %attend_project.1 = bf16[8,256,512]{2,1,0:T(8,128)(2,1)S(1)} custom-call(s32[64]{0:T(128)S(1)} %copy-done.3, s32[4]{0:T(128)S(1)} %copy-done, bf16[256,512]{1,0:T(8,128)(2,1)S(1)} %copy-done.2, bf16[512,128]{1,0:T(8,128)(2,1)S(1)} %constant_dynamic-update-slice_fusion.kv_ref, bf16[512,128]{1,0:T(8,128)(2,1)S(1)} %collective-permute-done.186.f0, ...), custom_call_target="tpu_custom_call" | custom-call | flops 3221225472 | bytes 8388608 | tf_op jit(solution)/shard_map/attend_project/pallas_call | solution.py:88
  140.4 34.5 %all_to_all.5.got_ref = bf16[8,256,512]{2,1,0:T(8,128)(2,1)S(1)} all-to-all(bf16[8,256,512]{2,1,0:T(8,128)(2,1)S(1)} %attend_project.1), channel_id=1, replica_groups=mesh['seq'=64,'head'=8] {'head'}, dimensions={0} | all-to-all | bytes 4194304 | tf_op jit(solution)/shard_map/all_to_all | solution.py:109
  174.9 1.6 add_shares.1
Async XLA Ops:
  1.7 117.2 %collective-permute-start.186 = (bf16[512,128]{1,0:T(8,128)(2,1)S(1)}, bf16[512,128]{1,0:T(8,128)(2,1)S(1)}, u32[]{:S(2)}, u32[]{:S(2)}) collective-permute-start(bf16[512,128]{1,0:T(8,128)(2,1)S(1)} %constant_dynamic-update-slice_fusion.kv_ref), channel_id=1, source_target_pairs={{0,504},{8,496},{16,488},{24,480},{32,472},{40,464},{48,456},{56,4... | collective-permute-start | bytes 393224 | tf_op jit(solution)/shard_map/ppermute | solution.py:73
  26.6 22.8 %collective-permute-start.154 = (bf16[512,128]{1,0:T(8,128)(2,1)S(1)}, bf16[512,128]{1,0:T(8,128)(2,1)}, u32[]{:S(2)}, u32[]{:S(2)}) collective-permute-start(bf16[512,128]{1,0:T(8,128)(2,1)S(1)} %param.154), channel_id=1, source_target_pairs={{0,248},{8,240},{16,232},{24,224},{32,216},{40,208},{48,200},{56,1... | collective-permute-start | bytes 393224 | tf_op jit(solution)/shard_map/cond/branch_30_fun/ppermute | solution.py:73
  49.3 28.0 %collective-permute-start.103 = (bf16[512,128]{1,0:T(8,128)(2,1)S(1)}, bf16[512,128]{1,0:T(8,128)(2,1)}, u32[]{:S(2)}, u32[]{:S(2)}) collective-permute-start(bf16[512,128]{1,0:T(8,128)(2,1)S(1)} %param.103), channel_id=1, source_target_pairs={{0,336},{8,344},{16,320},{24,328},{32,368},{40,376},{48,352},{56,3... | collective-permute-start | bytes 393224 | tf_op jit(solution)/shard_map/cond/branch_41_fun/ppermute | solution.py:73
  77.4 41.5 %collective-permute-start.37 = (bf16[512,128]{1,0:T(8,128)(2,1)S(1)}, bf16[512,128]{1,0:T(8,128)(2,1)}, u32[]{:S(2)}, u32[]{:S(2)}) collective-permute-start(bf16[512,128]{1,0:T(8,128)(2,1)S(1)} %param.37), channel_id=1, source_target_pairs={{0,304},{8,312},{16,288},{24,296},{32,272},{40,280},{48,256},{56,2... | collective-permute-start | bytes 393224 | tf_op jit(solution)/shard_map/cond/branch_37_fun/ppermute | solution.py:73
  118.9 0.7 copy-start
  119.5 2.2 %copy-start.1 = (bf16[512,4096]{1,0:T(8,128)(2,1)S(1)}, bf16[512,4096]{1,0:T(8,128)(2,1)}, u32[]{:S(2)}) copy-start(bf16[512,4096]{1,0:T(8,128)(2,1)} %w_ref.1) | copy-start | bytes 12582916
  121.7 0.9 copy-start.2
  122.7 0.7 copy-start.3

commit v2 on v1

--- a/solution.py
+++ b/solution.py
@@ -3,7 +3,7 @@
 from jax import lax
 from jax.experimental import pallas as pl
 from jax.experimental.pallas import tpu as pltpu
-from jax.sharding import PartitionSpec as P
+from jax.sharding import Mesh, PartitionSpec as P
 
 HD = 128
 GROUP = 4
@@ -13,7 +13,7 @@
 
 def attend_project(starts_ref, masks_ref, q_ref, kv_ref, f0, f1, f2, f3, w_ref, out_ref, peak, total, summed, attended):
     span = q_ref.shape[0]
-    me = lax.axis_index("seq")
+    me = lax.axis_index(("chip", "core"))
     own_start = starts_ref[me]
 
     def update(block, first, causal):
@@ -69,20 +69,50 @@
     out_ref[...] = acc.astype(out_ref.dtype)
 
 
-def permuted(mask):
-    return lambda x: lax.ppermute(x, "seq", [(i, i ^ mask) for i in range(lax.axis_size("seq"))])
+def stack_rows(key_ref, value_ref, out_ref):
+    span = key_ref.shape[0]
+    out_ref[0:span, :] = key_ref[...]
+    out_ref[span:, :] = value_ref[...]
+
+
+def pick_core(masks_ref, both_ref, *out_refs):
+    rows = out_refs[0].shape[0]
+    me = lax.axis_index("core")
+    for r, out_ref in enumerate(out_refs):
+        source = jnp.bitwise_xor(me, jnp.bitwise_and(masks_ref[r], 1))
+        out_ref[...] = both_ref[pl.ds(pl.multiple_of(source * rows, rows), rows), :]
+
+
+def swapped(mask):
+    if mask == 0:
+        return lambda x: x
+    return lambda x: lax.ppermute(x, "chip", [(i, i ^ mask) for i in range(lax.axis_size("chip"))])
 
 
 def per_device(query_rows, key_rows, value_rows, out_weight, span_starts, round_masks):
     span, width = query_rows.shape
     heads = lax.axis_size("head")
-    spans = lax.axis_size("seq")
+    chips = lax.axis_size("chip")
+    rounds = round_masks.shape[0]
     dout = out_weight.shape[1]
     cut = dout // heads
-    kv = jnp.concatenate([key_rows, value_rows], axis=0)
-    fars = [permuted(spans - 1)(kv)]
-    for r in range(1, round_masks.shape[0]):
-        fars.append(lax.switch(round_masks[r] - 1, [permuted(k) for k in range(1, spans - 1)], kv))
+    pair = jax.ShapeDtypeStruct((2 * span, HD), jnp.bfloat16)
+    kv = pl.pallas_call(stack_rows, out_shape=pair, name="stack_rows")(key_rows, value_rows)
+    both = lax.all_gather(kv, "core", tiled=True)
+    sends = pl.pallas_call(
+        pick_core,
+        grid_spec=pltpu.PrefetchScalarGridSpec(
+            num_scalar_prefetch=1,
+            grid=(1,),
+            in_specs=[pl.BlockSpec((4 * span, HD), lambda i, _: (0, 0))],
+            out_specs=[pl.BlockSpec((2 * span, HD), lambda i, _: (0, 0))] * rounds,
+        ),
+        out_shape=[pair] * rounds,
+        name="pick_core",
+    )(round_masks, both)
+    fars = [swapped(chips - 1)(sends[0])]
+    for r in range(1, rounds):
+        fars.append(lax.switch(round_masks[r] >> 1, [swapped(k) for k in range(chips)], sends[r]))
 
     whole = lambda shape: pl.BlockSpec(shape, lambda j, *_: (0,) * len(shape))
     shares = pl.pallas_call(
@@ -102,7 +132,7 @@
             ],
         ),
         out_shape=jax.ShapeDtypeStruct((heads, span, cut), jnp.bfloat16),
-        compiler_params=pltpu.CompilerParams(vmem_limit_bytes=32 * 2**20),
+        compiler_params=pltpu.CompilerParams(vmem_limit_bytes=58 * 2**20),
         cost_estimate=pl.CostEstimate(flops=3 * 2**30, bytes_accessed=8 * 2**20, transcendentals=2**21),
         name="attend_project",
     )(span_starts, round_masks, query_rows, kv, *fars, out_weight)
@@ -119,8 +149,10 @@
 
 
 def solution(mesh):
-    in_specs = (P("seq", "head"), P("seq", "head"), P("seq", "head"), P("head", None), P(), P())
-    out_specs = P("seq", "head")
+    seq, head = mesh.devices.shape
+    fine = Mesh(mesh.devices.reshape(seq // 2, 2, head), ("chip", "core", "head"))
+    rows = ("chip", "core")
+    in_specs = (P(rows, "head"), P(rows, "head"), P(rows, "head"), P("head", None), P(), P())
     return jax.shard_map(
-        per_device, mesh=mesh, in_specs=in_specs, out_specs=out_specs, check_vma=False
+        per_device, mesh=fine, in_specs=in_specs, out_specs=P(rows, "head"), check_vma=False
     )

time: 177 us -> 125 us (0.71)
  starting transfers between devices: 63.8 us -> 17.7 us
  waiting for transfers between devices: 50.1 us -> 34.9 us
  Pallas kernels: 18.7 us -> 26 us
  blocking collectives: 34.5 us -> 40.7 us
  local copies, waits for them, and re-layouts: 7.5 us -> 2.11 us
    ppermute x4, starting transfers between devices: 63.8 us -> 17.7 us  [swapped(): lax.ppermute(x, 'chip', [(i, i ^ mask) for i in range(lax.axis_size('chip...]
    ppermute x4, waiting for transfers between devices: 50.1 us -> 34.9 us  [swapped(): lax.ppermute(x, 'chip', [(i, i ^ mask) for i in range(lax.axis_size('chip...]
    all_gather x0 -> x1, blocking collectives: none -> 10.3 us  [per_device(): both = lax.all_gather(kv, 'core', tiled=True)]
    unnamed x9 -> x2, local copies, waits for them, and re-layouts: 5.29 us -> 0.65 us
    all_to_all x1, blocking collectives: 34.5 us -> 30.4 us  [per_device(): got = lax.all_to_all(shares, 'head', 0, 0, tiled=True)]
    pallas_call x0 -> x2, Pallas kernels: none -> 3.83 us  [the longest x1 2.29 us: per_device(): pl.pallas_call(pick_core, grid_spec=pltpu.PrefetchScalarGridSpec(num_scal...]
    pallas_call x1, Pallas kernels: 17.1 us -> 20.6 us  [per_device(): pl.pallas_call(attend_project, grid_spec=pltpu.PrefetchScalarGridSpec(num...]
where the time goes in v2:
time: 125 us; the launch traced here: 124 us
  blocking collectives  40.7 us (33%)
  waiting for transfers between devices  34.9 us (28%)
  Pallas kernels  26 us (21%)
  starting transfers between devices  17.7 us (14%)
  local copies, waits for them, and re-layouts  2.11 us (2%)
  between operations  1.92 us (2%)
    ppermute x4, waiting for transfers between devices, swapped(): lax.ppermute(x, 'chip', [(i, i ^ mask) for i in range(lax.axis_size('chip...  34.9 us
    all_to_all x1, blocking collectives, per_device(): got = lax.all_to_all(shares, 'head', 0, 0, tiled=True)  30.4 us
    pallas_call x1, Pallas kernels, per_device(): pl.pallas_call(attend_project, grid_spec=pltpu.PrefetchScalarGridSpec(num...  20.6 us
    ppermute x4, starting transfers between devices, swapped(): lax.ppermute(x, 'chip', [(i, i ^ mask) for i in range(lax.axis_size('chip...  17.7 us
    all_gather x1, blocking collectives, per_device(): both = lax.all_gather(kv, 'core', tiled=True)  10.3 us
  transfers between devices with their start and end apart: 4, of which 3 were waited for; matrix products, arithmetic and copies ran while one was open for 1% of the time, Pallas kernels for 0%

profile of v2, /device:TPU:1, one launch (start us, length us, event | category | flops | bytes accessed | tf_op | source)
XLA Modules:
  0.0 123.7 jit_solution(506031993943994848)
XLA Ops:
  0.0 1.5 %stack_rows.1.kv_ref = bf16[512,128]{1,0:T(8,128)(2,1)} custom-call(bf16[256,128]{1,0:T(8,128)(2,1)} %key_ref.1, bf16[256,128]{1,0:T(8,128)(2,1)} %value_ref.1), custom_call_target="tpu_custom_call" | custom-call | tf_op jit(solution)/shard_map/stack_rows/pallas_call | solution.py:100
  1.5 10.3 %all_gather.3.both_ref = bf16[1024,128]{1,0:T(8,128)(2,1)} all-gather(bf16[512,128]{1,0:T(8,128)(2,1)} %stack_rows.1.kv_ref), channel_id=1, replica_groups=mesh['chip'=32,'core'=2,'head'=8] {'core'}, dimensions={0}, use_global_device_ids=true | all-gather | bytes 393216 | tf_op jit(solution)/shard_map/all_gather | solution.py:101
  11.8 2.3 %pick_core.1 = (bf16[512,128]{1,0:T(8,128)(2,1)}, bf16[512,128]{1,0:T(8,128)(2,1)S(1)}, bf16[512,128]{1,0:T(8,128)(2,1)S(1)}, bf16[512,128]{1,0:T(8,128)(2,1)S(1)}) custom-call(s32[4]{0:T(128)} %masks_ref.3, bf16[1024,128]{1,0:T(8,128)(2,1)} %all_gather.3.both_ref), custom_call_target="tpu_custom_call" | custom-call | tf_op jit(solution)/shard_map/pick_core/pallas_call | solution.py:102
  14.1 6.7 %collective-permute-start.93 = (bf16[512,128]{1,0:T(8,128)(2,1)}, bf16[512,128]{1,0:T(8,128)(2,1)S(1)}, u32[]{:S(2)}, u32[]{:S(2)}) collective-permute-start(bf16[512,128]{1,0:T(8,128)(2,1)} %get-tuple-element.204), channel_id=1, source_target_pairs={{0,496},{16,480},{32,464},{48,448},{64,432},{80,416},{96,400},{112... | collective-permute-start | bytes 393224 | tf_op jit(solution)/shard_map/ppermute | solution.py:89
  20.8 1.4 %fusion = (s32[1]{0:T(128)}, s32[1]{0:T(128)}, s32[1]{0:T(128)}) fusion(s32[4]{0:T(128)} %masks_ref.3), kind=kLoop, calls=%fused_computation | loop fusion | bytes 24 | tf_op jit(solution)/shard_map/slice | solution.py:115
  24.1 19.3 %conditional.3 = (bf16[512,128]{1,0:T(8,128)(2,1)S(1)}) conditional(s32[]{:T(128)} %bitcast, bf16[512,128]{1,0:T(8,128)(2,1)S(1)} %get-tuple-element.205, bf16[512,128]{1,0:T(8,128)(2,1)S(1)} %get-tuple-element.205, bf16[512,128]{1,0:T(8,128)(2,1)S(1)} %get-tuple-element.205, ...), branch_computations={%region_0.0_spmd, %region_1.0_spmd, %region_2.0_spmd, %region_3.0_... | conditional | bytes 786480 | solution.py:115
  24.2 1.9 %collective-permute-start.25 = (bf16[512,128]{1,0:T(8,128)(2,1)S(1)}, bf16[512,128]{1,0:T(8,128)(2,1)S(1)}, u32[]{:S(2)}, u32[]{:S(2)}) collective-permute-start(bf16[512,128]{1,0:T(8,128)(2,1)S(1)} %param.26), channel_id=1, source_target_pairs={{0,416},{16,432},{32,384},{48,400},{64,480},{80,496},{96,448},{112... | collective-permute-start | bytes 393224 | tf_op jit(solution)/shard_map/cond/branch_26_fun/ppermute | solution.py:89
  26.1 17.3 %collective-permute-done.25 = bf16[512,128]{1,0:T(8,128)(2,1)S(1)} collective-permute-done((bf16[512,128]{1,0:T(8,128)(2,1)S(1)}, bf16[512,128]{1,0:T(8,128)(2,1)S(1)}, u32[]{:S(2)}, u32[]{:S(2)}) %collective-permute-start.25) | collective-permute-done | bytes 131104 | tf_op jit(solution)/shard_map/cond/branch_26_fun/ppermute | solution.py:89
  43.5 15.4 %conditional.4 = (bf16[512,128]{1,0:T(8,128)(2,1)S(1)}) conditional(s32[]{:T(128)} %bitcast.1, bf16[512,128]{1,0:T(8,128)(2,1)S(1)} %get-tuple-element.206, bf16[512,128]{1,0:T(8,128)(2,1)S(1)} %get-tuple-element.206, bf16[512,128]{1,0:T(8,128)(2,1)S(1)} %get-tuple-element.206, ...), branch_computations={%region_32.0_spmd, %region_33.0_spmd, %region_34.0_spmd, %region_3... | conditional | bytes 786480 | solution.py:115
  43.5 3.8 %collective-permute-start.54 = (bf16[512,128]{1,0:T(8,128)(2,1)S(1)}, bf16[512,128]{1,0:T(8,128)(2,1)S(1)}, u32[]{:S(2)}, u32[]{:S(2)}) collective-permute-start(bf16[512,128]{1,0:T(8,128)(2,1)S(1)} %param.56), channel_id=1, source_target_pairs={{0,384},{16,400},{32,416},{48,432},{64,448},{80,464},{96,480},{112... | collective-permute-start | bytes 393224 | tf_op jit(solution)/shard_map/cond/branch_24_fun/ppermute | solution.py:89
  47.3 11.5 %collective-permute-done.54 = bf16[512,128]{1,0:T(8,128)(2,1)S(1)} collective-permute-done((bf16[512,128]{1,0:T(8,128)(2,1)S(1)}, bf16[512,128]{1,0:T(8,128)(2,1)S(1)}, u32[]{:S(2)}, u32[]{:S(2)}) %collective-permute-start.54) | collective-permute-done | bytes 131104 | tf_op jit(solution)/shard_map/cond/branch_24_fun/ppermute | solution.py:89
  58.9 11.5 %conditional.5 = (bf16[512,128]{1,0:T(8,128)(2,1)S(1)}) conditional(s32[]{:T(128)} %bitcast.2, bf16[512,128]{1,0:T(8,128)(2,1)S(1)} %get-tuple-element.207, bf16[512,128]{1,0:T(8,128)(2,1)S(1)} %get-tuple-element.207, bf16[512,128]{1,0:T(8,128)(2,1)S(1)} %get-tuple-element.207, ...), branch_computations={%region_64.0_spmd, %region_65.0_spmd, %region_66.0_spmd, %region_6... | conditional | bytes 786480 | solution.py:115
  58.9 5.2 %collective-permute-start.66 = (bf16[512,128]{1,0:T(8,128)(2,1)S(1)}, bf16[512,128]{1,0:T(8,128)(2,1)S(1)}, u32[]{:S(2)}, u32[]{:S(2)}) collective-permute-start(bf16[512,128]{1,0:T(8,128)(2,1)S(1)} %param.69), channel_id=1, source_target_pairs={{0,80},{16,64},{32,112},{48,96},{64,16},{80,0},{96,48},{112,32},{1... | collective-permute-start | bytes 393224 | tf_op jit(solution)/shard_map/cond/branch_5_fun/ppermute | solution.py:89
  64.2 6.0 %collective-permute-done.66 = bf16[512,128]{1,0:T(8,128)(2,1)S(1)} collective-permute-done((bf16[512,128]{1,0:T(8,128)(2,1)S(1)}, bf16[512,128]{1,0:T(8,128)(2,1)S(1)}, u32[]{:S(2)}, u32[]{:S(2)}) %collective-permute-start.66) | collective-permute-done | bytes 131104 | tf_op jit(solution)/shard_map/cond/branch_5_fun/ppermute | solution.py:89
  70.4 0.0 collective-permute-done.93.f0
  70.4 0.0 copy-start
  70.4 0.7 copy-done
  71.1 20.6 %attend_project.1 = bf16[8,256,512]{2,1,0:T(8,128)(2,1)} custom-call(s32[64]{0:T(128)} %starts_ref.1, s32[4]{0:T(128)} %masks_ref.3, bf16[256,512]{1,0:T(8,128)(2,1)} %q_ref.1, bf16[512,128]{1,0:T(8,128)(2,1)} %stack_rows.1.kv_ref, bf16[512,128]{1,0:T(8,128)(2,1)} %copy-done, bf16[512,128]{1,0:T(8,128)(2,1)S(1)} %get-tuple-element.211.f1, ...), custom_call_target="tpu_custom_call" | custom-call | flops 3221225472 | bytes 8388608 | tf_op jit(solution)/shard_map/attend_project/pallas_call | solution.py:118
  91.7 30.4 %all_to_all.5.got_ref = bf16[8,256,512]{2,1,0:T(8,128)(2,1)S(1)} all-to-all(bf16[8,256,512]{2,1,0:T(8,128)(2,1)} %attend_project.1), channel_id=1, replica_groups=mesh['chip'=32,'core'=2,'head'=8] {'head'}, dimensions={0} | all-to-all | bytes 4194304 | tf_op jit(solution)/shard_map/all_to_all | solution.py:139
  122.1 1.6 %add_shares.1 = bf16[256,512]{1,0:T(8,128)(2,1)} custom-call(bf16[8,256,512]{2,1,0:T(8,128)(2,1)S(1)} %all_to_all.5.got_ref), custom_call_target="tpu_custom_call" | custom-call | tf_op jit(solution)/shard_map/add_shares/pallas_call | solution.py:140
  (3 shorter events, 0.0 us)
Async XLA Ops:
  14.1 56.3 %collective-permute-start.93 = (bf16[512,128]{1,0:T(8,128)(2,1)}, bf16[512,128]{1,0:T(8,128)(2,1)S(1)}, u32[]{:S(2)}, u32[]{:S(2)}) collective-permute-start(bf16[512,128]{1,0:T(8,128)(2,1)} %get-tuple-element.204), channel_id=1, source_target_pairs={{0,496},{16,480},{32,464},{48,448},{64,432},{80,416},{96,400},{112... | collective-permute-start | bytes 393224 | tf_op jit(solution)/shard_map/ppermute | solution.py:89
  24.2 19.2 %collective-permute-start.25 = (bf16[512,128]{1,0:T(8,128)(2,1)S(1)}, bf16[512,128]{1,0:T(8,128)(2,1)S(1)}, u32[]{:S(2)}, u32[]{:S(2)}) collective-permute-start(bf16[512,128]{1,0:T(8,128)(2,1)S(1)} %param.26), channel_id=1, source_target_pairs={{0,416},{16,432},{32,384},{48,400},{64,480},{80,496},{96,448},{112... | collective-permute-start | bytes 393224 | tf_op jit(solution)/shard_map/cond/branch_26_fun/ppermute | solution.py:89
  43.5 15.3 %collective-permute-start.54 = (bf16[512,128]{1,0:T(8,128)(2,1)S(1)}, bf16[512,128]{1,0:T(8,128)(2,1)S(1)}, u32[]{:S(2)}, u32[]{:S(2)}) collective-permute-start(bf16[512,128]{1,0:T(8,128)(2,1)S(1)} %param.56), channel_id=1, source_target_pairs={{0,384},{16,400},{32,416},{48,432},{64,448},{80,464},{96,480},{112... | collective-permute-start | bytes 393224 | tf_op jit(solution)/shard_map/cond/branch_24_fun/ppermute | solution.py:89
  58.9 11.3 %collective-permute-start.66 = (bf16[512,128]{1,0:T(8,128)(2,1)S(1)}, bf16[512,128]{1,0:T(8,128)(2,1)S(1)}, u32[]{:S(2)}, u32[]{:S(2)}) collective-permute-start(bf16[512,128]{1,0:T(8,128)(2,1)S(1)} %param.69), channel_id=1, source_target_pairs={{0,80},{16,64},{32,112},{48,96},{64,16},{80,0},{96,48},{112,32},{1... | collective-permute-start | bytes 393224 | tf_op jit(solution)/shard_map/cond/branch_5_fun/ppermute | solution.py:89
  70.4 0.7 copy-start

commit v3 on v1

v3 whole, which is shorter than its diff:
```python
import jax
import jax.numpy as jnp
from jax import lax
from jax.experimental import pallas as pl
from jax.experimental.pallas import tpu as pltpu
from jax.sharding import Mesh, PartitionSpec as P

HD = 128
GROUP = 4
FAR_BELOW = -1e30
SCALE = HD ** (-0.5) * 1.4426950408889634


def attend_project(
    starts_ref, masks_ref, q_ref, kv_ref, f0, f1, f2, f3, w_hbm, out_hbm, attended, w_ref, out_ref, w_sem, out_sem
):
    span = q_ref.shape[0]
    parts, _, cut = out_ref.shape
    w_copies = [
        pltpu.make_async_copy(w_hbm.at[:, pl.ds(j * cut, cut)], w_ref.at[j], w_sem.at[j]) for j in range(parts)
    ]
    for copy in w_copies:
        copy.start()
    me = lax.axis_index(("chip", "core"))
    own_start = starts_ref[me]
    blocks = [kv_ref, f0, f1, f2, f3]
    hidden = [0.0]
    for r in range(len(blocks) - 1):
        partner = jnp.bitwise_xor(me, masks_ref[r])
        hidden.append(jnp.where(starts_ref[partner] < own_start, 0.0, -FAR_BELOW))
    key = lax.broadcasted_iota(jnp.int32, (span, span), 0)
    token = lax.broadcasted_iota(jnp.int32, (span, span), 1)
    for h in range(GROUP):
        q = q_ref[:, h * HD : (h + 1) * HD]
        scores, peak = [], None
        for b, block in enumerate(blocks):
            part = lax.dot_general(
                block[0:span, :], q, (((1,), (1,)), ((), ())), preferred_element_type=jnp.float32
            )
            if b == 0:
                part = jnp.where(key <= token, part, FAR_BELOW)
            part_peak = jnp.max(part, axis=0, keepdims=True) * SCALE - hidden[b]
            peak = part_peak if b == 0 else jnp.maximum(peak, part_peak)
            scores.append(part)
        total, summed = 0.0, 0.0
        for b, block in enumerate(blocks):
            weights = jnp.exp2(scores[b] * SCALE - (peak + hidden[b]))
            total = total + jnp.sum(weights, axis=0, keepdims=True)
            summed = summed + lax.dot_general(
                block[span : 2 * span, :],
                weights.astype(jnp.bfloat16),
                (((0,), (0,)), ((), ())),
                preferred_element_type=jnp.float32,
            )
        attended[:, h * HD : (h + 1) * HD] = jnp.transpose(summed / total).astype(jnp.bfloat16)
    out_copies = []
    for j in range(parts):
        w_copies[j].wait()
        out_ref[j] = jnp.dot(attended[...], w_ref[j], preferred_element_type=jnp.float32).astype(jnp.bfloat16)
        out_copies.append(pltpu.make_async_copy(out_ref.at[j], out_hbm.at[j], out_sem.at[j]))
        out_copies[j].start()
    for copy in out_copies:
        copy.wait()


def add_shares(got_ref, out_ref):
    acc = got_ref[0].astype(jnp.float32)
    for j in range(1, got_ref.shape[0]):
        acc = acc + got_ref[j].astype(jnp.float32)
    out_ref[...] = acc.astype(out_ref.dtype)


def stack_rows(key_ref, value_ref, out_ref):
    span = key_ref.shape[0]
    out_ref[0:span, :] = key_ref[...]
    out_ref[span:, :] = value_ref[...]


def sent(mask):
    def send(own, other):
        block = other if mask & 1 else own
        if mask >> 1 == 0:
            return block
        return lax.ppermute(block, "chip", [(i, i ^ (mask >> 1)) for i in range(lax.axis_size("chip"))])

    return send


def per_device(query_rows, key_rows, value_rows, out_weight, span_starts, round_masks):
    span, width = query_rows.shape
    heads = lax.axis_size("head")
    spans = 2 * lax.axis_size("chip")
    cut = out_weight.shape[1] // heads
    kv = pl.pallas_call(
        stack_rows, out_shape=jax.ShapeDtypeStruct((2 * span, HD), jnp.bfloat16), name="stack_rows"
    )(key_rows, value_rows)
    other = lax.ppermute(kv, "core", [(0, 1), (1, 0)])
    fars = [sent(spans - 1)(kv, other)]
    for r in range(1, round_masks.shape[0]):
        fars.append(lax.switch(round_masks[r], [sent(k) for k in range(spans)], kv, other))

    vmem = pl.BlockSpec(memory_space=pltpu.VMEM)
    smem = pl.BlockSpec(memory_space=pltpu.SMEM)
    anywhere = pl.BlockSpec(memory_space=pl.ANY)
    shares = pl.pallas_call(
        attend_project,
        in_specs=[smem] * 2 + [vmem] * 6 + [anywhere],
        out_specs=anywhere,
        out_shape=jax.ShapeDtypeStruct((heads, span, cut), jnp.bfloat16),
        scratch_shapes=[
            pltpu.VMEM((span, width), jnp.bfloat16),
            pltpu.VMEM((heads, width, cut), jnp.bfloat16),
            pltpu.VMEM((heads, span, cut), jnp.bfloat16),
            pltpu.SemaphoreType.DMA((heads,)),
            pltpu.SemaphoreType.DMA((heads,)),
        ],
        compiler_params=pltpu.CompilerParams(vmem_limit_bytes=56 * 2**20),
        cost_estimate=pl.CostEstimate(flops=3 * 2**30, bytes_accessed=8 * 2**20, transcendentals=2**21),
        name="attend_project",
    )(span_starts, round_masks, query_rows, kv, *fars, out_weight)
    got = lax.all_to_all(shares, "head", 0, 0, tiled=True)
    return pl.pallas_call(
        add_shares,
        grid=(4,),
        in_specs=[pl.BlockSpec((heads, span // 4, cut), lambda j: (0, j, 0))],
        out_specs=pl.BlockSpec((span // 4, cut), lambda j: (j, 0)),
        out_shape=jax.ShapeDtypeStruct((span, cut), jnp.bfloat16),
        compiler_params=pltpu.CompilerParams(vmem_limit_bytes=32 * 2**20),
        name="add_shares",
    )(got)


def solution(mesh):
    seq, head = mesh.devices.shape
    fine = Mesh(mesh.devices.reshape(seq // 2, 2, head), ("chip", "core", "head"))
    rows = ("chip", "core")
    in_specs = (P(rows, "head"), P(rows, "head"), P(rows, "head"), P("head", None), P(), P())
    return jax.shard_map(
        per_device, mesh=fine, in_specs=in_specs, out_specs=P(rows, "head"), check_vma=False
    )
```

time: 177 us -> 114 us (0.64)
  starting transfers between devices: 63.8 us -> 27.1 us
  waiting for transfers between devices: 50.1 us -> 39 us
  Pallas kernels: 18.7 us -> 9.8 us
  local copies, waits for them, and re-layouts: 7.5 us -> 2.06 us
    ppermute x4 -> x5, starting transfers between devices: 63.8 us -> 27.1 us  [the longest x4 18.3 us: send(): lax.ppermute(block, 'chip', [(i, i ^ mask >> 1) for i in range(lax.axis_s...]
    ppermute x4 -> x5, waiting for transfers between devices: 50.1 us -> 39 us  [the longest x4 37.9 us: send(): lax.ppermute(block, 'chip', [(i, i ^ mask >> 1) for i in range(lax.axis_s...]
    pallas_call x1 -> x2, Pallas kernels: 17.1 us -> 8.2 us  [the longest x1 7.32 us: per_device(): pl.pallas_call(attend_project, in_specs=[smem] * 2 + [vmem] * 6 + [anywhe...]
    unnamed x9 -> x2, local copies, waits for them, and re-layouts: 5.29 us -> 0.66 us
  transfers between devices with their start and end apart: 4 -> 5, of which waited for: 3 -> 4; matrix products, arithmetic and copies ran while one was open for 1% -> 1% of each run, Pallas kernels for 0% -> 0%
where the time goes in v3:
time: 114 us
  waiting for transfers between devices  39 us (34%)
  blocking collectives  34 us (30%)
  starting transfers between devices  27.1 us (24%)
  Pallas kernels  9.8 us (9%)
  local copies, waits for them, and re-layouts  2.06 us (2%)
  between operations  1.88 us (2%)
    ppermute x4, waiting for transfers between devices, send(): lax.ppermute(block, 'chip', [(i, i ^ mask >> 1) for i in range(lax.axis_s...  37.9 us
    all_to_all x1, blocking collectives, per_device(): got = lax.all_to_all(shares, 'head', 0, 0, tiled=True)  34 us
    ppermute x4, starting transfers between devices, send(): lax.ppermute(block, 'chip', [(i, i ^ mask >> 1) for i in range(lax.axis_s...  18.3 us
    ppermute x1, starting transfers between devices, per_device(): other = lax.ppermute(kv, 'core', [(0, 1), (1, 0)])  8.79 us
    pallas_call x1, Pallas kernels, per_device(): pl.pallas_call(attend_project, in_specs=[smem] * 2 + [vmem] * 6 + [anywhe...  7.32 us
  transfers between devices with their start and end apart: 5, of which 4 were waited for; matrix products, arithmetic and copies ran while one was open for 1% of the time, Pallas kernels for 0%

profile of v3, /device:TPU:1, one launch (start us, length us, event | category | flops | bytes accessed | tf_op | source)
XLA Modules:
  0.0 113.9 jit_solution(13619748409071625504)
XLA Ops:
  0.0 0.9 stack_rows.1.kv_ref
  0.9 8.8 %collective-permute-start.186 = (bf16[512,128]{1,0:T(8,128)(2,1)S(1)}, bf16[512,128]{1,0:T(8,128)(2,1)}, u32[]{:S(2)}, u32[]{:S(2)}) collective-permute-start(bf16[512,128]{1,0:T(8,128)(2,1)S(1)} %stack_rows.1.kv_ref), channel_id=1, source_target_pairs={{0,8},{8,0},{1,9},{9,1},{2,10},{10,2},{3,11},{11,3},{4,12},{12,4},... | collective-permute-start | bytes 393224 | tf_op jit(solution)/shard_map/ppermute | solution.py:97
  9.7 1.1 collective-permute-done.186
  10.8 6.7 %collective-permute-start.187 = (bf16[512,128]{1,0:T(8,128)(2,1)}, bf16[512,128]{1,0:T(8,128)(2,1)S(1)}, u32[]{:S(2)}, u32[]{:S(2)}) collective-permute-start(bf16[512,128]{1,0:T(8,128)(2,1)} %collective-permute-done.186), channel_id=1, source_target_pairs={{0,496},{16,480},{32,464},{48,448},{64,432},{80,416},{96,400},{112... | collective-permute-start | bytes 393224 | tf_op jit(solution)/shard_map/ppermute | solution.py:84
  17.5 1.4 %fusion = (s32[1]{0:T(128)}, s32[1]{0:T(128)}, s32[1]{0:T(128)}) fusion(s32[4]{0:T(128)} %masks_ref.1), kind=kLoop, calls=%fused_computation | loop fusion | bytes 24 | tf_op jit(solution)/shard_map/slice | solution.py:100
  20.8 19.7 %conditional.5 = (bf16[512,128]{1,0:T(8,128)(2,1)}) conditional(s32[]{:T(128)} %bitcast.2, bf16[512,128]{1,0:T(8,128)(2,1)S(1)} %stack_rows.1.kv_ref, bf16[512,128]{1,0:T(8,128)(2,1)} %collective-permute-done.186, bf16[512,128]{1,0:T(8,128)(2,1)S(1)} %stack_rows.1.kv_ref, ...), branch_computations={%region_128.0_spmd, %region_129.0_spmd, %region_130.0_spmd, %regio... | conditional | bytes 524336 | solution.py:100
  20.8 7.8 %collective-permute-start.140 = (bf16[512,128]{1,0:T(8,128)(2,1)S(1)}, bf16[512,128]{1,0:T(8,128)(2,1)}, u32[]{:S(2)}, u32[]{:S(2)}) collective-permute-start(bf16[512,128]{1,0:T(8,128)(2,1)S(1)} %param.146), channel_id=1, source_target_pairs={{0,144},{16,128},{32,176},{48,160},{64,208},{80,192},{96,240},{112... | collective-permute-start | bytes 393224 | tf_op jit(solution)/shard_map/cond/branch_18_fun/ppermute | solution.py:84
  28.6 11.9 %collective-permute-done.140 = bf16[512,128]{1,0:T(8,128)(2,1)} collective-permute-done((bf16[512,128]{1,0:T(8,128)(2,1)S(1)}, bf16[512,128]{1,0:T(8,128)(2,1)}, u32[]{:S(2)}, u32[]{:S(2)}) %collective-permute-start.140) | collective-permute-done | bytes 131104 | tf_op jit(solution)/shard_map/cond/branch_18_fun/ppermute | solution.py:84
  40.5 21.1 %conditional.4 = (bf16[512,128]{1,0:T(8,128)(2,1)}) conditional(s32[]{:T(128)} %bitcast.1, bf16[512,128]{1,0:T(8,128)(2,1)S(1)} %stack_rows.1.kv_ref, bf16[512,128]{1,0:T(8,128)(2,1)} %collective-permute-done.186, bf16[512,128]{1,0:T(8,128)(2,1)S(1)} %stack_rows.1.kv_ref, ...), branch_computations={%region_64.0_spmd, %region_65.0_spmd, %region_66.0_spmd, %region_6... | conditional | bytes 524336 | solution.py:100
  40.5 1.9 %collective-permute-start.104 = (bf16[512,128]{1,0:T(8,128)(2,1)S(1)}, bf16[512,128]{1,0:T(8,128)(2,1)}, u32[]{:S(2)}, u32[]{:S(2)}) collective-permute-start(bf16[512,128]{1,0:T(8,128)(2,1)S(1)} %param.108), channel_id=1, source_target_pairs={{0,352},{16,368},{32,320},{48,336},{64,288},{80,304},{96,256},{112... | collective-permute-start | bytes 393224 | tf_op jit(solution)/shard_map/cond/branch_44_fun/ppermute | solution.py:84
  42.4 19.2 %collective-permute-done.104 = bf16[512,128]{1,0:T(8,128)(2,1)} collective-permute-done((bf16[512,128]{1,0:T(8,128)(2,1)S(1)}, bf16[512,128]{1,0:T(8,128)(2,1)}, u32[]{:S(2)}, u32[]{:S(2)}) %collective-permute-start.104) | collective-permute-done | bytes 131104 | tf_op jit(solution)/shard_map/cond/branch_44_fun/ppermute | solution.py:84
  61.6 8.8 %conditional.3 = (bf16[512,128]{1,0:T(8,128)(2,1)}) conditional(s32[]{:T(128)} %bitcast, bf16[512,128]{1,0:T(8,128)(2,1)S(1)} %stack_rows.1.kv_ref, bf16[512,128]{1,0:T(8,128)(2,1)} %collective-permute-done.186, bf16[512,128]{1,0:T(8,128)(2,1)S(1)} %stack_rows.1.kv_ref, ...), branch_computations={%region_0.0_spmd, %region_1.0_spmd, %region_2.0_spmd, %region_3.0_... | conditional | bytes 524336 | solution.py:100
  61.6 1.9 %collective-permute-start.6 = (bf16[512,128]{1,0:T(8,128)(2,1)S(1)}, bf16[512,128]{1,0:T(8,128)(2,1)}, u32[]{:S(2)}, u32[]{:S(2)}) collective-permute-start(bf16[512,128]{1,0:T(8,128)(2,1)S(1)} %param.8), channel_id=1, source_target_pairs={{0,64},{16,80},{32,96},{48,112},{64,0},{80,16},{96,32},{112,48},{1... | collective-permute-start | bytes 393224 | tf_op jit(solution)/shard_map/cond/branch_8_fun/ppermute | solution.py:84
  63.5 6.9 %collective-permute-done.6 = bf16[512,128]{1,0:T(8,128)(2,1)} collective-permute-done((bf16[512,128]{1,0:T(8,128)(2,1)S(1)}, bf16[512,128]{1,0:T(8,128)(2,1)}, u32[]{:S(2)}, u32[]{:S(2)}) %collective-permute-start.6) | collective-permute-done | bytes 131104 | tf_op jit(solution)/shard_map/cond/branch_8_fun/ppermute | solution.py:84
  70.3 0.0 collective-permute-done.187.f0
  70.3 0.0 copy-start
  70.4 0.7 copy-done
  71.0 7.3 %attend_project.1 = bf16[8,256,512]{2,1,0:T(8,128)(2,1)} custom-call(s32[64]{0:T(128)} %starts_ref.1, s32[4]{0:T(128)} %masks_ref.1, bf16[256,512]{1,0:T(8,128)(2,1)} %q_ref.1, bf16[512,128]{1,0:T(8,128)(2,1)S(1)} %stack_rows.1.kv_ref, bf16[512,128]{1,0:T(8,128)(2,1)} %copy-done, bf16[512,128]{1,0:T(8,128)(2,1)} %get-tuple-element.395.f1, ...), custom_call_target="tpu_custom_call" | custom-call | flops 3221225472 | bytes 8388608 | tf_op jit(solution)/shard_map/attend_project/pallas_call | solution.py:105
  78.3 34.0 %all_to_all.5.got_ref = bf16[8,256,512]{2,1,0:T(8,128)(2,1)S(1)} all-to-all(bf16[8,256,512]{2,1,0:T(8,128)(2,1)} %attend_project.1), channel_id=1, replica_groups=mesh['chip'=32,'core'=2,'head'=8] {'head'}, dimensions={0} | all-to-all | bytes 4194304 | tf_op jit(solution)/shard_map/all_to_all | solution.py:121
  112.3 1.6 %add_shares.1 = bf16[256,512]{1,0:T(8,128)(2,1)} custom-call(bf16[8,256,512]{2,1,0:T(8,128)(2,1)S(1)} %all_to_all.5.got_ref), custom_call_target="tpu_custom_call" | custom-call | tf_op jit(solution)/shard_map/add_shares/pallas_call | solution.py:122
Async XLA Ops:
  0.9 9.9 %collective-permute-start.186 = (bf16[512,128]{1,0:T(8,128)(2,1)S(1)}, bf16[512,128]{1,0:T(8,128)(2,1)}, u32[]{:S(2)}, u32[]{:S(2)}) collective-permute-start(bf16[512,128]{1,0:T(8,128)(2,1)S(1)} %stack_rows.1.kv_ref), channel_id=1, source_target_pairs={{0,8},{8,0},{1,9},{9,1},{2,10},{10,2},{3,11},{11,3},{4,12},{12,4},... | collective-permute-start | bytes 393224 | tf_op jit(solution)/shard_map/ppermute | solution.py:97
  10.8 59.6 %collective-permute-start.187 = (bf16[512,128]{1,0:T(8,128)(2,1)}, bf16[512,128]{1,0:T(8,128)(2,1)S(1)}, u32[]{:S(2)}, u32[]{:S(2)}) collective-permute-start(bf16[512,128]{1,0:T(8,128)(2,1)} %collective-permute-done.186), channel_id=1, source_target_pairs={{0,496},{16,480},{32,464},{48,448},{64,432},{80,416},{96,400},{112... | collective-permute-start | bytes 393224 | tf_op jit(solution)/shard_map/ppermute | solution.py:84
  20.8 19.6 %collective-permute-start.140 = (bf16[512,128]{1,0:T(8,128)(2,1)S(1)}, bf16[512,128]{1,0:T(8,128)(2,1)}, u32[]{:S(2)}, u32[]{:S(2)}) collective-permute-start(bf16[512,128]{1,0:T(8,128)(2,1)S(1)} %param.146), channel_id=1, source_target_pairs={{0,144},{16,128},{32,176},{48,160},{64,208},{80,192},{96,240},{112... | collective-permute-start | bytes 393224 | tf_op jit(solution)/shard_map/cond/branch_18_fun/ppermute | solution.py:84
  40.5 21.1 %collective-permute-start.104 = (bf16[512,128]{1,0:T(8,128)(2,1)S(1)}, bf16[512,128]{1,0:T(8,128)(2,1)}, u32[]{:S(2)}, u32[]{:S(2)}) collective-permute-start(bf16[512,128]{1,0:T(8,128)(2,1)S(1)} %param.108), channel_id=1, source_target_pairs={{0,352},{16,368},{32,320},{48,336},{64,288},{80,304},{96,256},{112... | collective-permute-start | bytes 393224 | tf_op jit(solution)/shard_map/cond/branch_44_fun/ppermute | solution.py:84
  61.6 8.8 %collective-permute-start.6 = (bf16[512,128]{1,0:T(8,128)(2,1)S(1)}, bf16[512,128]{1,0:T(8,128)(2,1)}, u32[]{:S(2)}, u32[]{:S(2)}) collective-permute-start(bf16[512,128]{1,0:T(8,128)(2,1)S(1)} %param.8), channel_id=1, source_target_pairs={{0,64},{16,80},{32,96},{48,112},{64,0},{80,16},{96,32},{112,48},{1... | collective-permute-start | bytes 393224 | tf_op jit(solution)/shard_map/cond/branch_8_fun/ppermute | solution.py:84
  70.3 0.7 copy-start

commit v4 on v3

--- a/solution.py
+++ b/solution.py
@@ -9,6 +9,13 @@
 GROUP = 4
 FAR_BELOW = -1e30
 SCALE = HD ** (-0.5) * 1.4426950408889634
+
+
+def in_order(masks):
+    a, b, c = masks[1], masks[2], masks[3]
+    low = jnp.minimum(jnp.minimum(a, b), c)
+    high = jnp.maximum(jnp.maximum(a, b), c)
+    return low, a + b + c - low - high, high
 
 
 def attend_project(
@@ -25,8 +32,8 @@
     own_start = starts_ref[me]
     blocks = [kv_ref, f0, f1, f2, f3]
     hidden = [0.0]
-    for r in range(len(blocks) - 1):
-        partner = jnp.bitwise_xor(me, masks_ref[r])
+    for mask in (masks_ref[0], *in_order(masks_ref)):
+        partner = jnp.bitwise_xor(me, mask)
         hidden.append(jnp.where(starts_ref[partner] < own_start, 0.0, -FAR_BELOW))
     key = lax.broadcasted_iota(jnp.int32, (span, span), 0)
     token = lax.broadcasted_iota(jnp.int32, (span, span), 1)
@@ -70,20 +77,41 @@
     out_ref[...] = acc.astype(out_ref.dtype)
 
 
-def stack_rows(key_ref, value_ref, out_ref):
+def prepare(masks_ref, key_ref, value_ref, kv_ref, low_ref, middle_ref, high_ref):
     span = key_ref.shape[0]
-    out_ref[0:span, :] = key_ref[...]
-    out_ref[span:, :] = value_ref[...]
+    low_ref[0], middle_ref[0], high_ref[0] = in_order(masks_ref)
+    kv_ref[0:span, :] = key_ref[...]
+    kv_ref[span:, :] = value_ref[...]
 
 
-def sent(mask):
-    def send(own, other):
-        block = other if mask & 1 else own
-        if mask >> 1 == 0:
-            return block
-        return lax.ppermute(block, "chip", [(i, i ^ (mask >> 1)) for i in range(lax.axis_size("chip"))])
+def across_chips(block, mask):
+    if mask == 0:
+        return block
+    return lax.ppermute(block, "chip", [(i, i ^ mask) for i in range(lax.axis_size("chip"))])
 
-    return send
+
+def across_cores(block):
+    return lax.ppermute(block, "core", [(0, 1), (1, 0)])
+
+
+def direct(mask):
+    return lambda own, other, *_: across_chips(other if mask & 1 else own, mask >> 1)
+
+
+def by_mirror(mask, last):
+    rest = mask ^ last
+
+    def fetch(own, other, mirrored):
+        block = across_cores(mirrored) if rest & 1 else mirrored
+        return across_chips(block, rest >> 1)
+
+    return fetch
+
+
+def nearer(mask, spans):
+    if mask & 1:
+        return mask >= spans * 11 // 16 or spans // 2 <= mask < spans * 5 // 8
+    return mask >= spans * 7 // 8
 
 
 def per_device(query_rows, key_rows, value_rows, out_weight, span_starts, round_masks):
@@ -91,17 +119,26 @@
     heads = lax.axis_size("head")
     spans = 2 * lax.axis_size("chip")
     cut = out_weight.shape[1] // heads
-    kv = pl.pallas_call(
-        stack_rows, out_shape=jax.ShapeDtypeStruct((2 * span, HD), jnp.bfloat16), name="stack_rows"
-    )(key_rows, value_rows)
-    other = lax.ppermute(kv, "core", [(0, 1), (1, 0)])
-    fars = [sent(spans - 1)(kv, other)]
-    for r in range(1, round_masks.shape[0]):
-        fars.append(lax.switch(round_masks[r], [sent(k) for k in range(spans)], kv, other))
-
     vmem = pl.BlockSpec(memory_space=pltpu.VMEM)
     smem = pl.BlockSpec(memory_space=pltpu.SMEM)
     anywhere = pl.BlockSpec(memory_space=pl.ANY)
+    scalar = jax.ShapeDtypeStruct((1,), jnp.int32)
+    kv, low, middle, high = pl.pallas_call(
+        prepare,
+        in_specs=[smem, vmem, vmem],
+        out_specs=[vmem, smem, smem, smem],
+        out_shape=[jax.ShapeDtypeStruct((2 * span, HD), jnp.bfloat16), scalar, scalar, scalar],
+        name="prepare",
+    )(round_masks, key_rows, value_rows)
+    last = spans - 1
+    mirrored = lax.ppermute(kv, ("chip", "core"), [(i, i ^ last) for i in range(spans)])
+    other = across_cores(kv)
+    plain = [direct(k) for k in range(spans)]
+    mixed = [by_mirror(k, last) if nearer(k, spans) else direct(k) for k in range(spans)]
+    first = lax.switch(low[0], plain, kv, other)
+    second = lax.switch(middle[0], mixed, kv, other, mirrored)
+    third = lax.switch(high[0], mixed, kv, other, mirrored)
+    fars = (mirrored, first, second, third)
     shares = pl.pallas_call(
         attend_project,
         in_specs=[smem] * 2 + [vmem] * 6 + [anywhere],

time: 114 us -> 100 us (0.88)
  the two profiles are of different devices: /device:TPU:1 before, /device:TPU:32 now
where the time goes in v4:
time: 100 us; the launch traced here: 99.8 us
  blocking collectives  35.3 us (35%)
  waiting for transfers between devices  29.4 us (29%)
  starting transfers between devices  22.8 us (23%)
  Pallas kernels  10.4 us (10%)
  between operations  1.91 us (2%)
    all_to_all x1, blocking collectives, per_device(): got = lax.all_to_all(shares, 'head', 0, 0, tiled=True)  35.3 us
    ppermute x3, waiting for transfers between devices, across_chips(): lax.ppermute(block, 'chip', [(i, i ^ mask) for i in range(lax.axis_size('...  29.4 us
    ppermute x1, starting transfers between devices, per_device(): lax.ppermute(kv, ('chip', 'core'), [(i, i ^ last) for i in range(spans)])  12.5 us
    ppermute x3, starting transfers between devices, across_chips(): lax.ppermute(block, 'chip', [(i, i ^ mask) for i in range(lax.axis_size('...  8.42 us
    pallas_call x1, Pallas kernels, per_device(): pl.pallas_call(attend_project, in_specs=[smem] * 2 + [vmem] * 6 + [anywhe...  7.34 us
  transfers between devices with their start and end apart: 5, of which 3 were waited for; matrix products, arithmetic and copies ran while one was open for 0% of the time, Pallas kernels for 0%

profile of v4, /device:TPU:32, one launch (start us, length us, event | category | flops | bytes accessed | tf_op | source)
XLA Modules:
  0.0 99.8 jit_solution(6382866774302764103)
XLA Ops:
  0.0 1.4 %prepare.1 = (bf16[512,128]{1,0:T(8,128)(2,1)S(1)}, s32[1]{0:T(128)}, s32[1]{0:T(128)}, s32[1]{0:T(128)}) custom-call(s32[4]{0:T(128)} %masks_ref.3, bf16[256,128]{1,0:T(8,128)(2,1)} %key_ref.1, bf16[256,128]{1,0:T(8,128)(2,1)} %value_ref.1), custom_call_target="tpu_custom_call" | custom-call | tf_op jit(solution)/shard_map/prepare/pallas_call | solution.py:126
  1.4 1.9 %collective-permute-start.191 = (bf16[512,128]{1,0:T(8,128)(2,1)S(1)}, bf16[512,128]{1,0:T(8,128)(2,1)S(1)}, u32[]{:S(2)}, u32[]{:S(2)}) collective-permute-start(bf16[512,128]{1,0:T(8,128)(2,1)S(1)} %get-tuple-element.396.kv_ref), channel_id=1, source_target_pairs={{0,8},{8,0},{1,9},{9,1},{2,10},{10,2},{3,11},{11,3},{4,12},{12,4},... | collective-permute-start | bytes 393224 | tf_op jit(solution)/shard_map/ppermute | solution.py:94
  3.4 12.5 %collective-permute-start.190 = (bf16[512,128]{1,0:T(8,128)(2,1)S(1)}, bf16[512,128]{1,0:T(8,128)(2,1)S(1)}, u32[]{:S(2)}, u32[]{:S(2)}) collective-permute-start(bf16[512,128]{1,0:T(8,128)(2,1)S(1)} %get-tuple-element.396.kv_ref), channel_id=1, source_target_pairs={{0,504},{8,496},{16,488},{24,480},{32,472},{40,464},{48,456},{56,4... | collective-permute-start | bytes 393224 | tf_op jit(solution)/shard_map/ppermute | solution.py:134
  17.7 0.0 collective-permute-done.191
  17.8 9.8 %conditional.3 = (bf16[512,128]{1,0:T(8,128)(2,1)}) conditional(s32[]{:T(128)} %bitcast, bf16[512,128]{1,0:T(8,128)(2,1)S(1)} %get-tuple-element.396.kv_ref, bf16[512,128]{1,0:T(8,128)(2,1)S(1)} %collective-permute-done.191, bf16[512,128]{1,0:T(8,128)(2,1)S(1)} %get-tuple-element.396.kv_ref, ...), branch_computations={%region_0.0_spmd, %region_1.0_spmd, %region_2.0_spmd, %region_3.0_... | conditional | bytes 524336 | solution.py:138
  17.8 2.0 %collective-permute-start.2 = (bf16[512,128]{1,0:T(8,128)(2,1)S(1)}, bf16[512,128]{1,0:T(8,128)(2,1)}, u32[]{:S(2)}, u32[]{:S(2)}) collective-permute-start(bf16[512,128]{1,0:T(8,128)(2,1)S(1)} %param.4), channel_id=1, source_target_pairs={{0,32},{16,48},{32,0},{48,16},{64,96},{80,112},{96,64},{112,80},{1... | collective-permute-start | bytes 393224 | tf_op jit(solution)/shard_map/cond/branch_4_fun/ppermute | solution.py:90
  19.8 7.7 %collective-permute-done.2 = bf16[512,128]{1,0:T(8,128)(2,1)} collective-permute-done((bf16[512,128]{1,0:T(8,128)(2,1)S(1)}, bf16[512,128]{1,0:T(8,128)(2,1)}, u32[]{:S(2)}, u32[]{:S(2)}) %collective-permute-start.2) | collective-permute-done | bytes 131104 | tf_op jit(solution)/shard_map/cond/branch_4_fun/ppermute | solution.py:90
  27.5 0.0 collective-permute-done.190.f0
  27.5 18.8 %conditional.5 = (bf16[512,128]{1,0:T(8,128)(2,1)}) conditional(s32[]{:T(128)} %bitcast.2, bf16[512,128]{1,0:T(8,128)(2,1)S(1)} %get-tuple-element.396.kv_ref, bf16[512,128]{1,0:T(8,128)(2,1)S(1)} %collective-permute-done.191, bf16[512,128]{1,0:T(8,128)(2,1)S(1)} %get-tuple-element.396.kv_ref, ...), branch_computations={%region_128.0_spmd, %region_129.0_spmd, %region_130.0_spmd, %regio... | conditional | bytes 1048664 | solution.py:140
  27.5 4.5 %collective-permute-start.144 = (bf16[512,128]{1,0:T(8,128)(2,1)S(1)}, bf16[512,128]{1,0:T(8,128)(2,1)}, u32[]{:S(2)}, u32[]{:S(2)}) collective-permute-start(bf16[512,128]{1,0:T(8,128)(2,1)S(1)} %param.148), channel_id=1, source_target_pairs={{0,160},{16,176},{32,128},{48,144},{64,224},{80,240},{96,192},{112... | collective-permute-start | bytes 393224 | tf_op jit(solution)/shard_map/cond/branch_20_fun/ppermute | solution.py:90
  32.0 14.3 %collective-permute-done.144 = bf16[512,128]{1,0:T(8,128)(2,1)} collective-permute-done((bf16[512,128]{1,0:T(8,128)(2,1)S(1)}, bf16[512,128]{1,0:T(8,128)(2,1)}, u32[]{:S(2)}, u32[]{:S(2)}) %collective-permute-start.144) | collective-permute-done | bytes 131104 | tf_op jit(solution)/shard_map/cond/branch_20_fun/ppermute | solution.py:90
  46.4 9.2 %conditional.4 = (bf16[512,128]{1,0:T(8,128)(2,1)}) conditional(s32[]{:T(128)} %bitcast.1, bf16[512,128]{1,0:T(8,128)(2,1)S(1)} %get-tuple-element.396.kv_ref, bf16[512,128]{1,0:T(8,128)(2,1)S(1)} %collective-permute-done.191, bf16[512,128]{1,0:T(8,128)(2,1)S(1)} %get-tuple-element.396.kv_ref, ...), branch_computations={%region_64.0_spmd, %region_65.0_spmd, %region_66.0_spmd, %region_6... | conditional | bytes 1048664 | solution.py:139
  46.4 1.9 %collective-permute-start.73 = (bf16[512,128]{1,0:T(8,128)(2,1)S(1)}, bf16[512,128]{1,0:T(8,128)(2,1)}, u32[]{:S(2)}, u32[]{:S(2)}) collective-permute-start(bf16[512,128]{1,0:T(8,128)(2,1)S(1)} %param.77), channel_id=1, source_target_pairs={{0,96},{16,112},{32,64},{48,80},{64,32},{80,48},{96,0},{112,16},{1... | collective-permute-start | bytes 393224 | tf_op jit(solution)/shard_map/cond/branch_13_fun/ppermute | solution.py:90
  48.3 7.3 %collective-permute-done.73 = bf16[512,128]{1,0:T(8,128)(2,1)} collective-permute-done((bf16[512,128]{1,0:T(8,128)(2,1)S(1)}, bf16[512,128]{1,0:T(8,128)(2,1)}, u32[]{:S(2)}, u32[]{:S(2)}) %collective-permute-start.73) | collective-permute-done | bytes 131104 | tf_op jit(solution)/shard_map/cond/branch_13_fun/ppermute | solution.py:90
  55.6 7.3 %attend_project.1 = bf16[8,256,512]{2,1,0:T(8,128)(2,1)} custom-call(s32[64]{0:T(128)} %starts_ref.1, s32[4]{0:T(128)} %masks_ref.3, bf16[256,512]{1,0:T(8,128)(2,1)} %q_ref.1, bf16[512,128]{1,0:T(8,128)(2,1)S(1)} %get-tuple-element.396.kv_ref, bf16[512,128]{1,0:T(8,128)(2,1)S(1)} %collective-permute-done.190.f0, bf16[512,128]{1,0:T(8,128)(2,1)} %get-tuple-element.400.f1, ...), custom_call_target="tpu_custom_call" | custom-call | flops 3221225472 | bytes 8388608 | tf_op jit(solution)/shard_map/attend_project/pallas_call | solution.py:142
  63.0 35.3 %all_to_all.5.got_ref = bf16[8,256,512]{2,1,0:T(8,128)(2,1)S(1)} all-to-all(bf16[8,256,512]{2,1,0:T(8,128)(2,1)} %attend_project.1), channel_id=1, replica_groups=mesh['chip'=32,'core'=2,'head'=8] {'head'}, dimensions={0} | all-to-all | bytes 4194304 | tf_op jit(solution)/shard_map/all_to_all | solution.py:158
  98.2 1.6 %add_shares.1 = bf16[256,512]{1,0:T(8,128)(2,1)} custom-call(bf16[8,256,512]{2,1,0:T(8,128)(2,1)S(1)} %all_to_all.5.got_ref), custom_call_target="tpu_custom_call" | custom-call | tf_op jit(solution)/shard_map/add_shares/pallas_call | solution.py:159
Async XLA Ops:
  1.4 16.3 %collective-permute-start.191 = (bf16[512,128]{1,0:T(8,128)(2,1)S(1)}, bf16[512,128]{1,0:T(8,128)(2,1)S(1)}, u32[]{:S(2)}, u32[]{:S(2)}) collective-permute-start(bf16[512,128]{1,0:T(8,128)(2,1)S(1)} %get-tuple-element.396.kv_ref), channel_id=1, source_target_pairs={{0,8},{8,0},{1,9},{9,1},{2,10},{10,2},{3,11},{11,3},{4,12},{12,4},... | collective-permute-start | bytes 393224 | tf_op jit(solution)/shard_map/ppermute | solution.py:94
  3.4 24.2 %collective-permute-start.190 = (bf16[512,128]{1,0:T(8,128)(2,1)S(1)}, bf16[512,128]{1,0:T(8,128)(2,1)S(1)}, u32[]{:S(2)}, u32[]{:S(2)}) collective-permute-start(bf16[512,128]{1,0:T(8,128)(2,1)S(1)} %get-tuple-element.396.kv_ref), channel_id=1, source_target_pairs={{0,504},{8,496},{16,488},{24,480},{32,472},{40,464},{48,456},{56,4... | collective-permute-start | bytes 393224 | tf_op jit(solution)/shard_map/ppermute | solution.py:134
  17.8 9.7 %collective-permute-start.2 = (bf16[512,128]{1,0:T(8,128)(2,1)S(1)}, bf16[512,128]{1,0:T(8,128)(2,1)}, u32[]{:S(2)}, u32[]{:S(2)}) collective-permute-start(bf16[512,128]{1,0:T(8,128)(2,1)S(1)} %param.4), channel_id=1, source_target_pairs={{0,32},{16,48},{32,0},{48,16},{64,96},{80,112},{96,64},{112,80},{1... | collective-permute-start | bytes 393224 | tf_op jit(solution)/shard_map/cond/branch_4_fun/ppermute | solution.py:90
  27.5 18.8 %collective-permute-start.144 = (bf16[512,128]{1,0:T(8,128)(2,1)S(1)}, bf16[512,128]{1,0:T(8,128)(2,1)}, u32[]{:S(2)}, u32[]{:S(2)}) collective-permute-start(bf16[512,128]{1,0:T(8,128)(2,1)S(1)} %param.148), channel_id=1, source_target_pairs={{0,160},{16,176},{32,128},{48,144},{64,224},{80,240},{96,192},{112... | collective-permute-start | bytes 393224 | tf_op jit(solution)/shard_map/cond/branch_20_fun/ppermute | solution.py:90
  46.4 9.2 %collective-permute-start.73 = (bf16[512,128]{1,0:T(8,128)(2,1)S(1)}, bf16[512,128]{1,0:T(8,128)(2,1)}, u32[]{:S(2)}, u32[]{:S(2)}) collective-permute-start(bf16[512,128]{1,0:T(8,128)(2,1)S(1)} %param.77), channel_id=1, source_target_pairs={{0,96},{16,112},{32,64},{48,80},{64,32},{80,48},{96,0},{112,16},{1... | collective-permute-start | bytes 393224 | tf_op jit(solution)/shard_map/cond/branch_13_fun/ppermute | solution.py:90

commit v5 on v4

--- a/solution.py
+++ b/solution.py
@@ -1,3 +1,5 @@
+import functools
+
 import jax
 import jax.numpy as jnp
 from jax import lax
@@ -37,7 +39,8 @@
         hidden.append(jnp.where(starts_ref[partner] < own_start, 0.0, -FAR_BELOW))
     key = lax.broadcasted_iota(jnp.int32, (span, span), 0)
     token = lax.broadcasted_iota(jnp.int32, (span, span), 1)
-    for h in range(GROUP):
+
+    def score(h):
         q = q_ref[:, h * HD : (h + 1) * HD]
         scores, peak = [], None
         for b, block in enumerate(blocks):
@@ -49,6 +52,12 @@
             part_peak = jnp.max(part, axis=0, keepdims=True) * SCALE - hidden[b]
             peak = part_peak if b == 0 else jnp.maximum(peak, part_peak)
             scores.append(part)
+        return scores, peak
+
+    ahead = score(0)
+    for h in range(GROUP):
+        scores, peak = ahead
+        ahead = score(h + 1) if h + 1 < GROUP else None
         total, summed = 0.0, 0.0
         for b, block in enumerate(blocks):
             weights = jnp.exp2(scores[b] * SCALE - (peak + hidden[b]))
@@ -59,7 +68,7 @@
                 (((0,), (0,)), ((), ())),
                 preferred_element_type=jnp.float32,
             )
-        attended[:, h * HD : (h + 1) * HD] = jnp.transpose(summed / total).astype(jnp.bfloat16)
+        attended[:, h * HD : (h + 1) * HD] = jnp.transpose(summed * (1.0 / total)).astype(jnp.bfloat16)
     out_copies = []
     for j in range(parts):
         w_copies[j].wait()
@@ -70,16 +79,21 @@
         copy.wait()
 
 
-def add_shares(got_ref, out_ref):
-    acc = got_ref[0].astype(jnp.float32)
-    for j in range(1, got_ref.shape[0]):
-        acc = acc + got_ref[j].astype(jnp.float32)
-    out_ref[...] = acc.astype(out_ref.dtype)
+def routes(masks, spans):
+    low, middle, high = in_order(masks)
+    shift = (spans // 4).bit_length() - 1
+
+    def after(mask, held):
+        quarter = mask >> shift
+        beside = (quarter == (held >> shift)) & (quarter > 0) & (quarter < 3)
+        return jnp.where(beside, spans + jnp.bitwise_xor(mask, held), mask)
+
+    return low, after(middle, low), after(high, middle)
 
 
-def prepare(masks_ref, key_ref, value_ref, kv_ref, low_ref, middle_ref, high_ref):
+def prepare(spans, masks_ref, key_ref, value_ref, kv_ref, low_ref, middle_ref, high_ref):
     span = key_ref.shape[0]
-    low_ref[0], middle_ref[0], high_ref[0] = in_order(masks_ref)
+    low_ref[0], middle_ref[0], high_ref[0] = routes(masks_ref, spans)
     kv_ref[0:span, :] = key_ref[...]
     kv_ref[span:, :] = value_ref[...]
 
@@ -98,14 +112,16 @@
     return lambda own, other, *_: across_chips(other if mask & 1 else own, mask >> 1)
 
 
-def by_mirror(mask, last):
-    rest = mask ^ last
+def onward(block, rest):
+    return across_chips(across_cores(block) if rest & 1 else block, rest >> 1)
 
-    def fetch(own, other, mirrored):
-        block = across_cores(mirrored) if rest & 1 else mirrored
-        return across_chips(block, rest >> 1)
 
-    return fetch
+def by_mirror(rest):
+    return lambda own, other, mirrored, *_: onward(mirrored, rest)
+
+
+def by_held(rest):
+    return lambda own, other, mirrored, held: onward(held, rest)
 
 
 def nearer(mask, spans):
@@ -114,31 +130,36 @@
     return mask >= spans * 7 // 8
 
 
+def fetch(kv, low, middle, high):
+    spans = 2 * lax.axis_size("chip")
+    last = spans - 1
+    mirrored = lax.ppermute(kv, ("chip", "core"), [(i, i ^ last) for i in range(spans)])
+    other = across_cores(kv)
+    plain = [direct(k) for k in range(spans)]
+    mixed = [by_mirror(k ^ last) if nearer(k, spans) else direct(k) for k in range(spans)]
+    mixed += [by_held(k) for k in range(spans // 4)]
+    first = lax.switch(low, plain, kv, other)
+    second = lax.switch(middle, mixed, kv, other, mirrored, first)
+    third = lax.switch(high, mixed, kv, other, mirrored, second)
+    return mirrored, first, second, third
+
+
 def per_device(query_rows, key_rows, value_rows, out_weight, span_starts, round_masks):
     span, width = query_rows.shape
     heads = lax.axis_size("head")
-    spans = 2 * lax.axis_size("chip")
     cut = out_weight.shape[1] // heads
     vmem = pl.BlockSpec(memory_space=pltpu.VMEM)
     smem = pl.BlockSpec(memory_space=pltpu.SMEM)
     anywhere = pl.BlockSpec(memory_space=pl.ANY)
     scalar = jax.ShapeDtypeStruct((1,), jnp.int32)
     kv, low, middle, high = pl.pallas_call(
-        prepare,
+        functools.partial(prepare, 2 * lax.axis_size("chip")),
         in_specs=[smem, vmem, vmem],
         out_specs=[vmem, smem, smem, smem],
         out_shape=[jax.ShapeDtypeStruct((2 * span, HD), jnp.bfloat16), scalar, scalar, scalar],
         name="prepare",
     )(round_masks, key_rows, value_rows)
-    last = spans - 1
-    mirrored = lax.ppermute(kv, ("chip", "core"), [(i, i ^ last) for i in range(spans)])
-    other = across_cores(kv)
-    plain = [direct(k) for k in range(spans)]
-    mixed = [by_mirror(k, last) if nearer(k, spans) else direct(k) for k in range(spans)]
-    first = lax.switch(low[0], plain, kv, other)
-    second = lax.switch(middle[0], mixed, kv, other, mirrored)
-    third = lax.switch(high[0], mixed, kv, other, mirrored)
-    fars = (mirrored, first, second, third)
+    fars = fetch(kv, low[0], middle[0], high[0])
     shares = pl.pallas_call(
         attend_project,
         in_specs=[smem] * 2 + [vmem] * 6 + [anywhere],
@@ -156,15 +177,7 @@
         name="attend_project",
     )(span_starts, round_masks, query_rows, kv, *fars, out_weight)
     got = lax.all_to_all(shares, "head", 0, 0, tiled=True)
-    return pl.pallas_call(
-        add_shares,
-        grid=(4,),
-        in_specs=[pl.BlockSpec((heads, span // 4, cut), lambda j: (0, j, 0))],
-        out_specs=pl.BlockSpec((span // 4, cut), lambda j: (j, 0)),
-        out_shape=jax.ShapeDtypeStruct((span, cut), jnp.bfloat16),
-        compiler_params=pltpu.CompilerParams(vmem_limit_bytes=32 * 2**20),
-        name="add_shares",
-    )(got)
+    return jnp.sum(got.astype(jnp.float32), axis=0).astype(jnp.bfloat16)
 
 
 def solution(mesh):

time: 100 us -> 94.3 us (0.943)
  the two profiles are of different devices: /device:TPU:32 before, /device:TPU:2 now
where the time goes in v5:
time: 94.3 us; the launch traced here: 93.9 us
  blocking collectives  32 us (34%)
  starting transfers between devices  26.6 us (28%)
  waiting for transfers between devices  24.1 us (26%)
  Pallas kernels  8.1 us (9%)
  between operations  2 us (2%)
  other arithmetic  1.05 us (1%)
    all_to_all x1, blocking collectives, per_device(): got = lax.all_to_all(shares, 'head', 0, 0, tiled=True)  32 us
    ppermute x3, waiting for transfers between devices, across_chips(): lax.ppermute(block, 'chip', [(i, i ^ mask) for i in range(lax.axis_size('...  24.1 us
    ppermute x1, starting transfers between devices, fetch(): lax.ppermute(kv, ('chip', 'core'), [(i, i ^ last) for i in range(spans)])  12.5 us
    ppermute x3, starting transfers between devices, across_chips(): lax.ppermute(block, 'chip', [(i, i ^ mask) for i in range(lax.axis_size('...  12.2 us
    pallas_call x1, Pallas kernels, per_device(): pl.pallas_call(attend_project, in_specs=[smem] * 2 + [vmem] * 6 + [anywhe...  6.68 us
    ppermute x1, starting transfers between devices, across_cores(): return lax.ppermute(block, 'core', [(0, 1), (1, 0)])  1.92 us
  transfers between devices with their start and end apart: 5, of which 3 were waited for; matrix products, arithmetic and copies ran while one was open for 0% of the time, Pallas kernels for 0%

profile of v5, /device:TPU:2, one launch (start us, length us, event | category | flops | bytes accessed | tf_op | source)
XLA Modules:
  0.0 93.9 jit_solution(8842469803742027626)
XLA Ops:
  0.0 1.4 %prepare.1 = (bf16[512,128]{1,0:T(8,128)(2,1)S(1)}, s32[1]{0:T(128)}, s32[1]{0:T(128)}, s32[1]{0:T(128)}) custom-call(s32[4]{0:T(128)} %masks_ref.3, bf16[256,128]{1,0:T(8,128)(2,1)} %key_ref.1, bf16[256,128]{1,0:T(8,128)(2,1)} %value_ref.1), custom_call_target="tpu_custom_call" | custom-call | tf_op jit(solution)/shard_map/prepare/pallas_call | solution.py:155
  1.4 1.9 %collective-permute-start.235 = (bf16[512,128]{1,0:T(8,128)(2,1)S(1)}, bf16[512,128]{1,0:T(8,128)(2,1)S(1)}, u32[]{:S(2)}, u32[]{:S(2)}) collective-permute-start(bf16[512,128]{1,0:T(8,128)(2,1)S(1)} %get-tuple-element.460.kv_ref), channel_id=1, source_target_pairs={{0,8},{8,0},{1,9},{9,1},{2,10},{10,2},{3,11},{11,3},{4,12},{12,4},... | collective-permute-start | bytes 393224 | tf_op jit(solution)/shard_map/ppermute | solution.py:108
  3.4 12.5 %collective-permute-start.234 = (bf16[512,128]{1,0:T(8,128)(2,1)S(1)}, bf16[512,128]{1,0:T(8,128)(2,1)S(1)}, u32[]{:S(2)}, u32[]{:S(2)}) collective-permute-start(bf16[512,128]{1,0:T(8,128)(2,1)S(1)} %get-tuple-element.460.kv_ref), channel_id=1, source_target_pairs={{0,504},{8,496},{16,488},{24,480},{32,472},{40,464},{48,456},{56,4... | collective-permute-start | bytes 393224 | tf_op jit(solution)/shard_map/ppermute | solution.py:136
  17.8 0.0 collective-permute-done.235
  17.9 20.4 %conditional.3 = (bf16[512,128]{1,0:T(8,128)(2,1)}) conditional(s32[]{:T(128)} %bitcast, bf16[512,128]{1,0:T(8,128)(2,1)S(1)} %get-tuple-element.460.kv_ref, bf16[512,128]{1,0:T(8,128)(2,1)S(1)} %collective-permute-done.235, bf16[512,128]{1,0:T(8,128)(2,1)S(1)} %get-tuple-element.460.kv_ref, ...), branch_computations={%region_0.0_spmd, %region_1.0_spmd, %region_2.0_spmd, %region_3.0_... | conditional | bytes 524336 | solution.py:141
  17.9 8.2 %collective-permute-start.15 = (bf16[512,128]{1,0:T(8,128)(2,1)S(1)}, bf16[512,128]{1,0:T(8,128)(2,1)}, u32[]{:S(2)}, u32[]{:S(2)}) collective-permute-start(bf16[512,128]{1,0:T(8,128)(2,1)S(1)} %param.17), channel_id=1, source_target_pairs={{0,128},{16,144},{32,160},{48,176},{64,192},{80,208},{96,224},{112... | collective-permute-start | bytes 393224 | tf_op jit(solution)/shard_map/cond/branch_17_fun/ppermute | solution.py:104
  26.1 12.2 %collective-permute-done.15 = bf16[512,128]{1,0:T(8,128)(2,1)} collective-permute-done((bf16[512,128]{1,0:T(8,128)(2,1)S(1)}, bf16[512,128]{1,0:T(8,128)(2,1)}, u32[]{:S(2)}, u32[]{:S(2)}) %collective-permute-start.15) | collective-permute-done | bytes 131104 | tf_op jit(solution)/shard_map/cond/branch_17_fun/ppermute | solution.py:104
  38.3 0.0 collective-permute-done.234.f0
  38.3 8.1 %conditional.4 = (bf16[512,128]{1,0:T(8,128)(2,1)}) conditional(s32[]{:T(128)} %bitcast.1, bf16[512,128]{1,0:T(8,128)(2,1)S(1)} %get-tuple-element.460.kv_ref, bf16[512,128]{1,0:T(8,128)(2,1)S(1)} %collective-permute-done.235, bf16[512,128]{1,0:T(8,128)(2,1)S(1)} %get-tuple-element.460.kv_ref, ...), branch_computations={%region_64.0_spmd, %region_65.0_spmd, %region_66.0_spmd, %region_6... | conditional | bytes 1048664 | solution.py:142
  38.3 1.9 %collective-permute-start.133 = (bf16[512,128]{1,0:T(8,128)(2,1)}, bf16[512,128]{1,0:T(8,128)(2,1)}, u32[]{:S(2)}, u32[]{:S(2)}) collective-permute-start(bf16[512,128]{1,0:T(8,128)(2,1)} %param.134), channel_id=1, source_target_pairs={{0,48},{16,32},{32,16},{48,0},{64,112},{80,96},{96,80},{112,64},{1... | collective-permute-start | bytes 393224 | tf_op jit(solution)/shard_map/cond/branch_70_fun/ppermute | solution.py:104
  40.2 6.1 %collective-permute-done.133 = bf16[512,128]{1,0:T(8,128)(2,1)} collective-permute-done((bf16[512,128]{1,0:T(8,128)(2,1)}, bf16[512,128]{1,0:T(8,128)(2,1)}, u32[]{:S(2)}, u32[]{:S(2)}) %collective-permute-start.133) | collective-permute-done | bytes 131104 | tf_op jit(solution)/shard_map/cond/branch_70_fun/ppermute | solution.py:104
  46.3 7.9 %conditional.5 = (bf16[512,128]{1,0:T(8,128)(2,1)}) conditional(s32[]{:T(128)} %bitcast.2, bf16[512,128]{1,0:T(8,128)(2,1)S(1)} %get-tuple-element.460.kv_ref, bf16[512,128]{1,0:T(8,128)(2,1)S(1)} %collective-permute-done.235, bf16[512,128]{1,0:T(8,128)(2,1)S(1)} %get-tuple-element.460.kv_ref, ...), branch_computations={%region_144.0_spmd, %region_145.0_spmd, %region_146.0_spmd, %regio... | conditional | bytes 1048664 | solution.py:143
  46.3 2.1 %collective-permute-start.204 = (bf16[512,128]{1,0:T(8,128)(2,1)S(1)}, bf16[512,128]{1,0:T(8,128)(2,1)}, u32[]{:S(2)}, u32[]{:S(2)}) collective-permute-start(bf16[512,128]{1,0:T(8,128)(2,1)S(1)} %param.201), channel_id=1, source_target_pairs={{0,48},{16,32},{32,16},{48,0},{64,112},{80,96},{96,80},{112,64},{1... | collective-permute-start | bytes 393224 | tf_op jit(solution)/shard_map/cond/branch_57_fun/ppermute | solution.py:104
  48.4 5.7 %collective-permute-done.204 = bf16[512,128]{1,0:T(8,128)(2,1)} collective-permute-done((bf16[512,128]{1,0:T(8,128)(2,1)S(1)}, bf16[512,128]{1,0:T(8,128)(2,1)}, u32[]{:S(2)}, u32[]{:S(2)}) %collective-permute-start.204) | collective-permute-done | bytes 131104 | tf_op jit(solution)/shard_map/cond/branch_57_fun/ppermute | solution.py:104
  54.2 6.7 %attend_project.1 = bf16[8,256,512]{2,1,0:T(8,128)(2,1)} custom-call(s32[64]{0:T(128)} %starts_ref.1, s32[4]{0:T(128)} %masks_ref.3, bf16[256,512]{1,0:T(8,128)(2,1)} %q_ref.1, bf16[512,128]{1,0:T(8,128)(2,1)S(1)} %get-tuple-element.460.kv_ref, bf16[512,128]{1,0:T(8,128)(2,1)S(1)} %collective-permute-done.234.f0, bf16[512,128]{1,0:T(8,128)(2,1)} %get-tuple-element.464.f1, ...), custom_call_target="tpu_custom_call" | custom-call | flops 3221225472 | bytes 8388608 | tf_op jit(solution)/shard_map/attend_project/pallas_call | solution.py:163
  60.9 32.0 %all_to_all.5 = bf16[8,256,512]{2,1,0:T(8,128)(2,1)S(1)} all-to-all(bf16[8,256,512]{2,1,0:T(8,128)(2,1)} %attend_project.1), channel_id=1, replica_groups=mesh['chip'=32,'core'=2,'head'=8] {'head'}, dimensions={0} | all-to-all | bytes 4194304 | tf_op jit(solution)/shard_map/all_to_all | solution.py:179
  92.9 1.0 %reduce_sum.12 = bf16[256,512]{1,0:T(8,128)(2,1)} reduce(bf16[8,256,512]{2,1,0:T(8,128)(2,1)S(1)} %all_to_all.5, bf16[]{:T(256)} %constant.14.clone.1), dimensions={0}, to_apply=%region_224.0 | reduce | flops 917504 | bytes 2359298 | tf_op jit(solution)/shard_map/reduce_sum | solution.py:180
Async XLA Ops:
  1.4 16.4 %collective-permute-start.235 = (bf16[512,128]{1,0:T(8,128)(2,1)S(1)}, bf16[512,128]{1,0:T(8,128)(2,1)S(1)}, u32[]{:S(2)}, u32[]{:S(2)}) collective-permute-start(bf16[512,128]{1,0:T(8,128)(2,1)S(1)} %get-tuple-element.460.kv_ref), channel_id=1, source_target_pairs={{0,8},{8,0},{1,9},{9,1},{2,10},{10,2},{3,11},{11,3},{4,12},{12,4},... | collective-permute-start | bytes 393224 | tf_op jit(solution)/shard_map/ppermute | solution.py:108
  3.4 34.9 %collective-permute-start.234 = (bf16[512,128]{1,0:T(8,128)(2,1)S(1)}, bf16[512,128]{1,0:T(8,128)(2,1)S(1)}, u32[]{:S(2)}, u32[]{:S(2)}) collective-permute-start(bf16[512,128]{1,0:T(8,128)(2,1)S(1)} %get-tuple-element.460.kv_ref), channel_id=1, source_target_pairs={{0,504},{8,496},{16,488},{24,480},{32,472},{40,464},{48,456},{56,4... | collective-permute-start | bytes 393224 | tf_op jit(solution)/shard_map/ppermute | solution.py:136
  17.9 20.4 %collective-permute-start.15 = (bf16[512,128]{1,0:T(8,128)(2,1)S(1)}, bf16[512,128]{1,0:T(8,128)(2,1)}, u32[]{:S(2)}, u32[]{:S(2)}) collective-permute-start(bf16[512,128]{1,0:T(8,128)(2,1)S(1)} %param.17), channel_id=1, source_target_pairs={{0,128},{16,144},{32,160},{48,176},{64,192},{80,208},{96,224},{112... | collective-permute-start | bytes 393224 | tf_op jit(solution)/shard_map/cond/branch_17_fun/ppermute | solution.py:104
  38.3 8.1 %collective-permute-start.133 = (bf16[512,128]{1,0:T(8,128)(2,1)}, bf16[512,128]{1,0:T(8,128)(2,1)}, u32[]{:S(2)}, u32[]{:S(2)}) collective-permute-start(bf16[512,128]{1,0:T(8,128)(2,1)} %param.134), channel_id=1, source_target_pairs={{0,48},{16,32},{32,16},{48,0},{64,112},{80,96},{96,80},{112,64},{1... | collective-permute-start | bytes 393224 | tf_op jit(solution)/shard_map/cond/branch_70_fun/ppermute | solution.py:104
  46.3 7.9 %collective-permute-start.204 = (bf16[512,128]{1,0:T(8,128)(2,1)S(1)}, bf16[512,128]{1,0:T(8,128)(2,1)}, u32[]{:S(2)}, u32[]{:S(2)}) collective-permute-start(bf16[512,128]{1,0:T(8,128)(2,1)S(1)} %param.201), channel_id=1, source_target_pairs={{0,48},{16,32},{32,16},{48,0},{64,112},{80,96},{96,80},{112,64},{1... | collective-permute-start | bytes 393224 | tf_op jit(solution)/shard_map/cond/branch_57_fun/ppermute | solution.py:104

commit v6 on v5

--- a/solution.py
+++ b/solution.py
@@ -13,11 +13,14 @@
 SCALE = HD ** (-0.5) * 1.4426950408889634
 
 
-def in_order(masks):
-    a, b, c = masks[1], masks[2], masks[3]
+def in_order(masks, spans):
+    def turned(mask):
+        return jnp.where(mask < spans // 2, jnp.bitwise_xor(mask, spans // 4), mask)
+
+    a, b, c = turned(masks[1]), turned(masks[2]), turned(masks[3])
     low = jnp.minimum(jnp.minimum(a, b), c)
     high = jnp.maximum(jnp.maximum(a, b), c)
-    return low, a + b + c - low - high, high
+    return turned(low), turned(a + b + c - low - high), turned(high)
 
 
 def attend_project(
@@ -34,7 +37,7 @@
     own_start = starts_ref[me]
     blocks = [kv_ref, f0, f1, f2, f3]
     hidden = [0.0]
-    for mask in (masks_ref[0], *in_order(masks_ref)):
+    for mask in (masks_ref[0], *in_order(masks_ref, starts_ref.shape[0])):
         partner = jnp.bitwise_xor(me, mask)
         hidden.append(jnp.where(starts_ref[partner] < own_start, 0.0, -FAR_BELOW))
     key = lax.broadcasted_iota(jnp.int32, (span, span), 0)
@@ -80,13 +83,16 @@
 
 
 def routes(masks, spans):
-    low, middle, high = in_order(masks)
-    shift = (spans // 4).bit_length() - 1
+    low, middle, high = in_order(masks, spans)
+    part = spans // 4
+    shift = part.bit_length() - 1
 
     def after(mask, held):
+        rest = jnp.bitwise_xor(mask, held)
         quarter = mask >> shift
-        beside = (quarter == (held >> shift)) & (quarter > 0) & (quarter < 3)
-        return jnp.where(beside, spans + jnp.bitwise_xor(mask, held), mask)
+        same = (quarter == (held >> shift)) & (quarter > 0) & (quarter < 3)
+        across = (quarter == 2) & ((held >> shift) == 1) & ((rest & 1) == 0)
+        return jnp.where(same, spans + rest, jnp.where(across, 2 * part + rest, mask))
 
     return low, after(middle, low), after(high, middle)
 
@@ -138,6 +144,7 @@
     plain = [direct(k) for k in range(spans)]
     mixed = [by_mirror(k ^ last) if nearer(k, spans) else direct(k) for k in range(spans)]
     mixed += [by_held(k) for k in range(spans // 4)]
+    mixed += [by_held(k) for k in range(spans * 3 // 4, spans)]
     first = lax.switch(low, plain, kv, other)
     second = lax.switch(middle, mixed, kv, other, mirrored, first)
     third = lax.switch(high, mixed, kv, other, mirrored, second)

time: 94.3 us -> 103 us (1.092)
  the two profiles are of different devices: /device:TPU:2 before, /device:TPU:8 now
where the time goes in v6:
time: 103 us
  blocking collectives  33.9 us (33%)
  waiting for transfers between devices  30.2 us (29%)
  starting transfers between devices  27.9 us (27%)
  Pallas kernels  8.1 us (8%)
  between operations  1.8 us (2%)
  other arithmetic  1.05 us (1%)
    all_to_all x1, blocking collectives, per_device(): got = lax.all_to_all(shares, 'head', 0, 0, tiled=True)  33.9 us
    ppermute x3, waiting for transfers between devices, across_chips(): lax.ppermute(block, 'chip', [(i, i ^ mask) for i in range(lax.axis_size('...  28.7 us
    ppermute x3, starting transfers between devices, across_chips(): lax.ppermute(block, 'chip', [(i, i ^ mask) for i in range(lax.axis_size('...  12.6 us
    ppermute x1, starting transfers between devices, fetch(): lax.ppermute(kv, ('chip', 'core'), [(i, i ^ last) for i in range(spans)])  11.4 us
    pallas_call x1, Pallas kernels, per_device(): pl.pallas_call(attend_project, in_specs=[smem] * 2 + [vmem] * 6 + [anywhe...  6.67 us
    ppermute x2, starting transfers between devices, across_cores(): return lax.ppermute(block, 'core', [(0, 1), (1, 0)])  3.83 us
  transfers between devices with their start and end apart: 6, of which 4 were waited for; matrix products, arithmetic and copies ran while one was open for 0% of the time, Pallas kernels for 0%

profile of v6, /device:TPU:8, one launch (start us, length us, event | category | flops | bytes accessed | tf_op | source)
XLA Modules:
  0.0 103.0 jit_solution(15856326591449934537)
XLA Ops:
  0.0 1.4 %prepare.1 = (bf16[512,128]{1,0:T(8,128)(2,1)S(1)}, s32[1]{0:T(128)}, s32[1]{0:T(128)}, s32[1]{0:T(128)}) custom-call(s32[4]{0:T(128)} %masks_ref.3, bf16[256,128]{1,0:T(8,128)(2,1)} %key_ref.1, bf16[256,128]{1,0:T(8,128)(2,1)} %value_ref.1), custom_call_target="tpu_custom_call" | custom-call | tf_op jit(solution)/shard_map/prepare/pallas_call | solution.py:162
  1.4 1.9 %collective-permute-start.283 = (bf16[512,128]{1,0:T(8,128)(2,1)S(1)}, bf16[512,128]{1,0:T(8,128)(2,1)S(1)}, u32[]{:S(2)}, u32[]{:S(2)}) collective-permute-start(bf16[512,128]{1,0:T(8,128)(2,1)S(1)} %get-tuple-element.524.kv_ref), channel_id=1, source_target_pairs={{0,8},{8,0},{1,9},{9,1},{2,10},{10,2},{3,11},{11,3},{4,12},{12,4},... | collective-permute-start | bytes 393224 | tf_op jit(solution)/shard_map/ppermute | solution.py:114
  3.4 11.4 %collective-permute-start.282 = (bf16[512,128]{1,0:T(8,128)(2,1)S(1)}, bf16[512,128]{1,0:T(8,128)(2,1)S(1)}, u32[]{:S(2)}, u32[]{:S(2)}) collective-permute-start(bf16[512,128]{1,0:T(8,128)(2,1)S(1)} %get-tuple-element.524.kv_ref), channel_id=1, source_target_pairs={{0,504},{8,496},{16,488},{24,480},{32,472},{40,464},{48,456},{56,4... | collective-permute-start | bytes 393224 | tf_op jit(solution)/shard_map/ppermute | solution.py:142
  16.5 0.0 collective-permute-done.283
  16.5 20.4 %conditional.3 = (bf16[512,128]{1,0:T(8,128)(2,1)}) conditional(s32[]{:T(128)} %bitcast, bf16[512,128]{1,0:T(8,128)(2,1)S(1)} %get-tuple-element.524.kv_ref, bf16[512,128]{1,0:T(8,128)(2,1)S(1)} %collective-permute-done.283, bf16[512,128]{1,0:T(8,128)(2,1)S(1)} %get-tuple-element.524.kv_ref, ...), branch_computations={%region_0.0_spmd, %region_1.0_spmd, %region_2.0_spmd, %region_3.0_... | conditional | bytes 524336 | solution.py:148
  16.6 8.2 %collective-permute-start.14 = (bf16[512,128]{1,0:T(8,128)(2,1)S(1)}, bf16[512,128]{1,0:T(8,128)(2,1)}, u32[]{:S(2)}, u32[]{:S(2)}) collective-permute-start(bf16[512,128]{1,0:T(8,128)(2,1)S(1)} %param.16), channel_id=1, source_target_pairs={{0,128},{16,144},{32,160},{48,176},{64,192},{80,208},{96,224},{112... | collective-permute-start | bytes 393224 | tf_op jit(solution)/shard_map/cond/branch_16_fun/ppermute | solution.py:110
  24.7 12.2 %collective-permute-done.14 = bf16[512,128]{1,0:T(8,128)(2,1)} collective-permute-done((bf16[512,128]{1,0:T(8,128)(2,1)S(1)}, bf16[512,128]{1,0:T(8,128)(2,1)}, u32[]{:S(2)}, u32[]{:S(2)}) %collective-permute-start.14) | collective-permute-done | bytes 131104 | tf_op jit(solution)/shard_map/cond/branch_16_fun/ppermute | solution.py:110
  36.9 0.0 collective-permute-done.282.f0
  36.9 11.0 %conditional.4 = (bf16[512,128]{1,0:T(8,128)(2,1)}) conditional(s32[]{:T(128)} %bitcast.1, bf16[512,128]{1,0:T(8,128)(2,1)S(1)} %get-tuple-element.524.kv_ref, bf16[512,128]{1,0:T(8,128)(2,1)S(1)} %collective-permute-done.283, bf16[512,128]{1,0:T(8,128)(2,1)S(1)} %get-tuple-element.524.kv_ref, ...), branch_computations={%region_64.0_spmd, %region_65.0_spmd, %region_66.0_spmd, %region_6... | conditional | bytes 1048664 | solution.py:149
  36.9 1.9 %collective-permute-start.131 = (bf16[512,128]{1,0:T(8,128)(2,1)}, bf16[512,128]{1,0:T(8,128)(2,1)S(1)}, u32[]{:S(2)}, u32[]{:S(2)}) collective-permute-start(bf16[512,128]{1,0:T(8,128)(2,1)} %param.133), channel_id=1, source_target_pairs={{0,8},{8,0},{1,9},{9,1},{2,10},{10,2},{3,11},{11,3},{4,12},{12,4},... | collective-permute-start | bytes 393224 | tf_op jit(solution)/shard_map/cond/branch_69_fun/ppermute | solution.py:114
  38.9 1.5 %collective-permute-done.131 = bf16[512,128]{1,0:T(8,128)(2,1)S(1)} collective-permute-done((bf16[512,128]{1,0:T(8,128)(2,1)}, bf16[512,128]{1,0:T(8,128)(2,1)S(1)}, u32[]{:S(2)}, u32[]{:S(2)}) %collective-permute-start.131) | collective-permute-done | bytes 131104 | tf_op jit(solution)/shard_map/cond/branch_69_fun/ppermute | solution.py:114
  40.4 1.9 %collective-permute-start.132 = (bf16[512,128]{1,0:T(8,128)(2,1)S(1)}, bf16[512,128]{1,0:T(8,128)(2,1)}, u32[]{:S(2)}, u32[]{:S(2)}) collective-permute-start(bf16[512,128]{1,0:T(8,128)(2,1)S(1)} %collective-permute-done.131), channel_id=1, source_target_pairs={{0,32},{16,48},{32,0},{48,16},{64,96},{80,112},{96,64},{112,80},{1... | collective-permute-start | bytes 393224 | tf_op jit(solution)/shard_map/cond/branch_69_fun/ppermute | solution.py:110
  42.3 5.6 %collective-permute-done.132 = bf16[512,128]{1,0:T(8,128)(2,1)} collective-permute-done((bf16[512,128]{1,0:T(8,128)(2,1)S(1)}, bf16[512,128]{1,0:T(8,128)(2,1)}, u32[]{:S(2)}, u32[]{:S(2)}) %collective-permute-start.132) | collective-permute-done | bytes 131104 | tf_op jit(solution)/shard_map/cond/branch_69_fun/ppermute | solution.py:110
  47.9 13.4 %conditional.5 = (bf16[512,128]{1,0:T(8,128)(2,1)}) conditional(s32[]{:T(128)} %bitcast.2, bf16[512,128]{1,0:T(8,128)(2,1)S(1)} %get-tuple-element.524.kv_ref, bf16[512,128]{1,0:T(8,128)(2,1)S(1)} %collective-permute-done.283, bf16[512,128]{1,0:T(8,128)(2,1)S(1)} %get-tuple-element.524.kv_ref, ...), branch_computations={%region_160.0_spmd, %region_161.0_spmd, %region_162.0_spmd, %regio... | conditional | bytes 1048664 | solution.py:150
  47.9 2.6 %collective-permute-start.224 = (bf16[512,128]{1,0:T(8,128)(2,1)S(1)}, bf16[512,128]{1,0:T(8,128)(2,1)}, u32[]{:S(2)}, u32[]{:S(2)}) collective-permute-start(bf16[512,128]{1,0:T(8,128)(2,1)S(1)} %param.214), channel_id=1, source_target_pairs={{0,432},{16,416},{32,400},{48,384},{64,496},{80,480},{96,464},{112... | collective-permute-start | bytes 393224 | tf_op jit(solution)/shard_map/cond/branch_54_fun/ppermute | solution.py:110
  50.5 10.8 %collective-permute-done.224 = bf16[512,128]{1,0:T(8,128)(2,1)} collective-permute-done((bf16[512,128]{1,0:T(8,128)(2,1)S(1)}, bf16[512,128]{1,0:T(8,128)(2,1)}, u32[]{:S(2)}, u32[]{:S(2)}) %collective-permute-start.224) | collective-permute-done | bytes 131104 | tf_op jit(solution)/shard_map/cond/branch_54_fun/ppermute | solution.py:110
  61.3 6.7 %attend_project.1 = bf16[8,256,512]{2,1,0:T(8,128)(2,1)} custom-call(s32[64]{0:T(128)} %starts_ref.1, s32[4]{0:T(128)} %masks_ref.3, bf16[256,512]{1,0:T(8,128)(2,1)} %q_ref.1, bf16[512,128]{1,0:T(8,128)(2,1)S(1)} %get-tuple-element.524.kv_ref, bf16[512,128]{1,0:T(8,128)(2,1)S(1)} %collective-permute-done.282.f0, bf16[512,128]{1,0:T(8,128)(2,1)} %get-tuple-element.528.f1, ...), custom_call_target="tpu_custom_call" | custom-call | flops 3221225472 | bytes 8388608 | tf_op jit(solution)/shard_map/attend_project/pallas_call | solution.py:170
  68.0 33.9 %all_to_all.5 = bf16[8,256,512]{2,1,0:T(8,128)(2,1)S(1)} all-to-all(bf16[8,256,512]{2,1,0:T(8,128)(2,1)} %attend_project.1), channel_id=1, replica_groups=mesh['chip'=32,'core'=2,'head'=8] {'head'}, dimensions={0} | all-to-all | bytes 4194304 | tf_op jit(solution)/shard_map/all_to_all | solution.py:186
  102.0 1.0 %reduce_sum.12 = bf16[256,512]{1,0:T(8,128)(2,1)} reduce(bf16[8,256,512]{2,1,0:T(8,128)(2,1)S(1)} %all_to_all.5, bf16[]{:T(256)} %constant.14.clone.1), dimensions={0}, to_apply=%region_256.0 | reduce | flops 917504 | bytes 2359298 | tf_op jit(solution)/shard_map/reduce_sum | solution.py:187
Async XLA Ops:
  1.4 15.1 %collective-permute-start.283 = (bf16[512,128]{1,0:T(8,128)(2,1)S(1)}, bf16[512,128]{1,0:T(8,128)(2,1)S(1)}, u32[]{:S(2)}, u32[]{:S(2)}) collective-permute-start(bf16[512,128]{1,0:T(8,128)(2,1)S(1)} %get-tuple-element.524.kv_ref), channel_id=1, source_target_pairs={{0,8},{8,0},{1,9},{9,1},{2,10},{10,2},{3,11},{11,3},{4,12},{12,4},... | collective-permute-start | bytes 393224 | tf_op jit(solution)/shard_map/ppermute | solution.py:114
  3.4 33.6 %collective-permute-start.282 = (bf16[512,128]{1,0:T(8,128)(2,1)S(1)}, bf16[512,128]{1,0:T(8,128)(2,1)S(1)}, u32[]{:S(2)}, u32[]{:S(2)}) collective-permute-start(bf16[512,128]{1,0:T(8,128)(2,1)S(1)} %get-tuple-element.524.kv_ref), channel_id=1, source_target_pairs={{0,504},{8,496},{16,488},{24,480},{32,472},{40,464},{48,456},{56,4... | collective-permute-start | bytes 393224 | tf_op jit(solution)/shard_map/ppermute | solution.py:142
  16.6 20.4 %collective-permute-start.14 = (bf16[512,128]{1,0:T(8,128)(2,1)S(1)}, bf16[512,128]{1,0:T(8,128)(2,1)}, u32[]{:S(2)}, u32[]{:S(2)}) collective-permute-start(bf16[512,128]{1,0:T(8,128)(2,1)S(1)} %param.16), channel_id=1, source_target_pairs={{0,128},{16,144},{32,160},{48,176},{64,192},{80,208},{96,224},{112... | collective-permute-start | bytes 393224 | tf_op jit(solution)/shard_map/cond/branch_16_fun/ppermute | solution.py:110
  36.9 3.4 %collective-permute-start.131 = (bf16[512,128]{1,0:T(8,128)(2,1)}, bf16[512,128]{1,0:T(8,128)(2,1)S(1)}, u32[]{:S(2)}, u32[]{:S(2)}) collective-permute-start(bf16[512,128]{1,0:T(8,128)(2,1)} %param.133), channel_id=1, source_target_pairs={{0,8},{8,0},{1,9},{9,1},{2,10},{10,2},{3,11},{11,3},{4,12},{12,4},... | collective-permute-start | bytes 393224 | tf_op jit(solution)/shard_map/cond/branch_69_fun/ppermute | solution.py:114
  40.4 7.5 %collective-permute-start.132 = (bf16[512,128]{1,0:T(8,128)(2,1)S(1)}, bf16[512,128]{1,0:T(8,128)(2,1)}, u32[]{:S(2)}, u32[]{:S(2)}) collective-permute-start(bf16[512,128]{1,0:T(8,128)(2,1)S(1)} %collective-permute-done.131), channel_id=1, source_target_pairs={{0,32},{16,48},{32,0},{48,16},{64,96},{80,112},{96,64},{112,80},{1... | collective-permute-start | bytes 393224 | tf_op jit(solution)/shard_map/cond/branch_69_fun/ppermute | solution.py:110
  47.9 13.4 %collective-permute-start.224 = (bf16[512,128]{1,0:T(8,128)(2,1)S(1)}, bf16[512,128]{1,0:T(8,128)(2,1)}, u32[]{:S(2)}, u32[]{:S(2)}) collective-permute-start(bf16[512,128]{1,0:T(8,128)(2,1)S(1)} %param.214), channel_id=1, source_target_pairs={{0,432},{16,416},{32,400},{48,384},{64,496},{80,480},{96,464},{112... | collective-permute-start | bytes 393224 | tf_op jit(solution)/shard_map/cond/branch_54_fun/ppermute | solution.py:110
